TPU v7x, 1024 devices: a whole 4x8x16 slice. The times are simulated.
1024 devices in a mesh: expert: 64 (over x, z), dp: 16 (over y, core).
Axes of the slice: x: 4, y: 8, z: 16, core: 2. Of those that a mesh axis runs over, the one named last changes fastest.
Arguments:
- latent: bfloat16 [131072, 1024], P(('expert', 'dp')), may hold values from -6 to 6
- cotangent: bfloat16 [131072, 1024], P(('expert', 'dp')), may hold values from -6 to 6
- routes: int32 [131072, 1], P(('expert', 'dp')), may hold values from 0 to 63; in each aligned block of 128 rows (0 to 127, 128 to 255, ...) at most 3 rows name the same one
- gates: float32 [131072, 1], P(('expert', 'dp')), may hold values from 0.25 to 1
- up_weight: bfloat16 [64, 1024, 2048], P('expert'), may hold values from -0.1875 to 0.1875
- down_weight: bfloat16 [64, 2048, 1024], P('expert'), may hold values from -0.125 to 0.125
Outputs:
- mixed: bfloat16 [131072, 1024], P(('expert', 'dp'))
- down_grad: bfloat16 [64, 2048, 1024], P('expert', 'dp')
Inputs may be any that keep to these rules, and one draw needn't show every extreme that they name: `routes`: in each aligned block of 128 rows (the tokens of one device) no expert is named by more than 3 rows, and in some blocks one expert is named by exactly 3 rows.
All inputs are finite; a program needn't handle non-finite values.
Results may differ from a plain program's by a relative error of at most 0.019.
Values may be sent and summed in bfloat16 or wider, within the bound.
No kernel may reach another device: no remote copies, remote signals or barrier semaphores. Data moves between devices by JAX's collectives and lax.ppermute only.
A program may use at most 64 MiB of HBM per device.

v0:
```python
import jax
import jax.numpy as jnp
from jax import lax
from jax.sharding import PartitionSpec as P


def on_device(latent, cotangent, routes, gates, up_weight, down_weight):
    expert_count = lax.axis_size("expert")
    group_count = lax.axis_size("dp")
    tok_rows, width = latent.shape
    route_count = routes.shape[1]
    hidden_width = up_weight.shape[2]
    capacity = max(2, 3 * tok_rows * route_count // (2 * expert_count))
    slots = expert_count * capacity
    factor = 1.0 / (tok_rows * route_count * group_count) ** 0.5
    route = routes[:, 0]
    onehot = (route[:, None] == jnp.arange(expert_count, dtype=jnp.int32)[None, :]).astype(
        jnp.int32
    )
    earlier = jnp.cumsum(onehot, axis=0) - onehot
    target = route * capacity + jnp.sum(earlier * onehot, axis=1)
    gate = gates[:, 0]
    weighted = (gate[:, None] * cotangent.astype(jnp.float32)).astype(jnp.bfloat16)
    blank = jnp.zeros((slots, width), jnp.bfloat16)
    send_rows = blank.at[target].set(latent).reshape(expert_count, capacity, width)
    send_cot = blank.at[target].set(weighted).reshape(expert_count, capacity, width)
    up_matrix = up_weight[0]
    down_matrix = down_weight[0]
    rows_in = lax.all_to_all(send_rows, "expert", split_axis=0, concat_axis=0, tiled=True)
    rows_cot = lax.all_to_all(send_cot, "expert", split_axis=0, concat_axis=0, tiled=True)
    per_source = rows_in.shape[1]
    flat_in = rows_in.reshape(-1, width)
    preact = jnp.dot(flat_in, up_matrix, preferred_element_type=jnp.float32)
    hidden = (jnp.maximum(preact, 0.0) ** 2).astype(jnp.bfloat16)
    expert_out = jnp.dot(hidden, down_matrix, preferred_element_type=jnp.float32).astype(
        jnp.bfloat16
    )
    expert_out, hidden, rows_cot = (
        expert_out.reshape(expert_count, per_source, width),
        hidden.reshape(expert_count, per_source, hidden_width),
        rows_cot,
    )
    returned = lax.all_to_all(expert_out, "expert", split_axis=0, concat_axis=0, tiled=True)
    token_out = returned.reshape(slots, width)[target]
    mixed = (gate[:, None] * token_out.astype(jnp.float32)).astype(jnp.bfloat16)
    hidden_flat = hidden.reshape(slots, hidden_width)
    cot_flat = rows_cot.reshape(slots, width)
    share = hidden_width // group_count
    columns = lax.all_to_all(hidden_flat, "dp", split_axis=1, concat_axis=0, tiled=True)
    piece = lax.all_gather(cot_flat, "dp", axis=0, tiled=True)
    groups = piece.shape[0] // slots
    product = jnp.einsum(
        "gsh,gsl->ghl",
        columns.reshape(groups, slots, share),
        piece.reshape(groups, slots, width),
        preferred_element_type=jnp.float32,
    )
    rounded = lax.optimization_barrier((factor * product).astype(jnp.bfloat16))
    summed = jnp.sum(rounded.astype(jnp.float32), axis=0)
    down_grad = summed.astype(jnp.bfloat16)[None]
    return (mixed, down_grad)


def solution(mesh):
    in_specs = (
        P(("expert", "dp"), None),
        P(("expert", "dp"), None),
        P(("expert", "dp"), None),
        P(("expert", "dp"), None),
        P("expert", None, None),
        P("expert", None, None),
    )
    out_specs = (P(("expert", "dp"), None), P("expert", "dp", None))
    return jax.shard_map(
        on_device, mesh=mesh, in_specs=in_specs, out_specs=out_specs, check_vma=False
    )
```

profile of v0, /device:TPU:1, one launch (start us, length us, event | category | flops | bytes accessed | tf_op | source)
XLA Modules:
  0.0 198.3 jit_solution(6881118568479508466)
XLA Ops:
  7.2 0.0 all-gather.2.cloned.1.call-start
  7.2 0.7 fusion.22
  8.0 0.2 reduce_window_sum.11
  8.1 0.8 select_reduce_fusion
  9.0 0.7 fusion.23
  9.6 1.7 scatter_custom_fusion.1
  11.4 0.2 reshape.35
  11.6 52.0 %all_to_all.31 = bf16[64,3,1024]{2,1,0:T(4,128)(2,1)S(1)} all-to-all(bf16[64,3,1024]{2,1,0:T(4,128)(2,1)S(1)} %reshape.35), channel_id=1, replica_groups=mesh['expert'=64,'dp'=16] {'expert'}, dimensions={0} | all-to-all | bytes 786432 | tf_op jit(solution)/shard_map/all_to_all | solution.py:30
  63.6 1.1 reshape.36
  64.7 0.0 all-gather.2.cloned.1.call-update
  64.7 1.7 scatter_custom_fusion
  66.4 0.2 reshape.31
  66.6 37.5 %all_to_all.32 = bf16[64,3,1024]{2,1,0:T(4,128)(2,1)S(1)} all-to-all(bf16[64,3,1024]{2,1,0:T(4,128)(2,1)S(1)} %reshape.31), channel_id=1, replica_groups=mesh['expert'=64,'dp'=16] {'expert'}, dimensions={0} | all-to-all | bytes 786432 | tf_op jit(solution)/shard_map/all_to_all | solution.py:29
  104.1 0.3 reshape.32
  104.5 0.0 copy-start.1
  104.5 3.4 %fusion.10 = bf16[192,2048]{1,0:T(8,128)(2,1)S(1)} fusion(bf16[192,1024]{1,0:T(8,128)(2,1)S(1)} %reshape.32, bf16[1,1024,2048]{2,1,0:T(8,128)(2,1)} %param.10), kind=kOutput, calls=%fused_computation.10 | convolution fusion | flops 806486016 | bytes 5373952 | tf_op jit(solution)/shard_map/dot_general | solution.py:33
  107.9 0.2 copy-done.1
  108.1 1.0 fusion.13
  109.1 0.0 copy-start
  109.1 1.0 reshape.33
  110.2 8.8 %all-to-all-start.1 = ((bf16[64,3,1024]{2,1,0:T(4,128)(2,1)}), bf16[64,3,1024]{2,1,0:T(4,128)(2,1)S(1)}, u32[]{:S(2)}, u32[]{:S(2)}) async-start(bf16[64,3,1024]{2,1,0:T(4,128)(2,1)} %reshape.33), calls=%async_computation.1 | async-start | bytes 1048576 | tf_op jit(solution)/shard_map/all_to_all | solution.py:43
  119.0 1.1 copy_bitcast_fusion
  120.1 28.0 %all-to-all-done.1 = bf16[64,3,1024]{2,1,0:T(4,128)(2,1)S(1)} async-done(((bf16[64,3,1024]{2,1,0:T(4,128)(2,1)}), bf16[64,3,1024]{2,1,0:T(4,128)(2,1)S(1)}, u32[]{:S(2)}, u32[]{:S(2)}) %all-to-all-start.1) | async-done | bytes 393248 | tf_op jit(solution)/shard_map/all_to_all | solution.py:43
  148.1 10.6 %all-to-all-start.2 = ((bf16[192,16,128]{2,0,1:T(8,128)(2,1)}), bf16[192,16,128]{2,0,1:T(8,128)(2,1)S(1)}, u32[]{:S(2)}, u32[]{:S(2)}) async-start(bf16[192,16,128]{2,0,1:T(8,128)(2,1)} %copy_bitcast_fusion), calls=%async_computation.2 | async-start | bytes 1572864 | tf_op jit(solution)/shard_map/all_to_all | solution.py:49
  158.7 0.3 reshape.34
  159.0 0.9 gather_fusion
  159.9 0.0 copy-done
  159.9 0.8 multiply_convert_fusion.2
  160.7 20.6 %all-to-all-done.2 = bf16[192,16,128]{2,0,1:T(8,128)(2,1)S(1)} async-done(((bf16[192,16,128]{2,0,1:T(8,128)(2,1)}), bf16[192,16,128]{2,0,1:T(8,128)(2,1)S(1)}, u32[]{:S(2)}, u32[]{:S(2)}) %all-to-all-start.2) | async-done | bytes 786464 | tf_op jit(solution)/shard_map/all_to_all | solution.py:49
  181.3 0.0 all-gather.2.cloned.1.call-done
  181.3 6.2 %multiply_convert_fusion = bf16[16,128,1024]{2,1,0:T(8,128)(2,1)} fusion(bf16[16,192,1024]{2,1,0:T(8,128)(2,1)} %bitcast.35, bf16[192,16,128]{2,0,1:T(8,128)(2,1)S(1)} %all-to-all-done.2), kind=kOutput, calls=%fused_computation.3 | convolution fusion | flops 809500672 | bytes 11272192 | tf_op jit(solution)/shard_map/gsh,gsl->ghl/dot_general | solution.py:52
  187.5 3.9 %reduce_sum.25 = bf16[128,1024]{1,0:T(8,128)(2,1)} reduce(bf16[16,128,1024]{2,1,0:T(8,128)(2,1)} %multiply_convert_fusion, bf16[]{:T(256)} %constant.6.clone.1), dimensions={0}, to_apply=%region_4.5 | reduce | flops 1966080 | bytes 4456450 | tf_op jit(solution)/shard_map/reduce_sum | solution.py:59
  (1 shorter events, 0.0 us)
Async XLA Ops:
  7.2 174.2 %all-gather.2.cloned.1.call-start = ((), (), s32[]{:S(2)}) async-start(), calls=%async_computation.4 | async-start | bytes 6684672 | tf_op jit(solution)/shard_map/all_gather | solution.py:50
  104.5 3.6 %copy-start.1 = (bf16[1,2048,1024]{2,1,0:T(8,128)(2,1)S(1)}, bf16[1,2048,1024]{2,1,0:T(8,128)(2,1)}, u32[]{:S(2)}) copy-start(bf16[1,2048,1024]{2,1,0:T(8,128)(2,1)} %param.11) | copy-start | bytes 12582916
  109.1 50.7 %copy-start = (f32[128,1]{0,1:T(1,128)S(1)}, f32[128,1]{0,1:T(1,128)}, u32[]{:S(2)}) copy-start(f32[128,1]{0,1:T(1,128)} %param.9) | copy-start | bytes 1540
  110.2 37.9 %all-to-all-start.1 = ((bf16[64,3,1024]{2,1,0:T(4,128)(2,1)}), bf16[64,3,1024]{2,1,0:T(4,128)(2,1)S(1)}, u32[]{:S(2)}, u32[]{:S(2)}) async-start(bf16[64,3,1024]{2,1,0:T(4,128)(2,1)} %reshape.33), calls=%async_computation.1 | async-start | bytes 1048576 | tf_op jit(solution)/shard_map/all_to_all | solution.py:43
  148.1 33.3 %all-to-all-start.2 = ((bf16[192,16,128]{2,0,1:T(8,128)(2,1)}), bf16[192,16,128]{2,0,1:T(8,128)(2,1)S(1)}, u32[]{:S(2)}, u32[]{:S(2)}) async-start(bf16[192,16,128]{2,0,1:T(8,128)(2,1)} %copy_bitcast_fusion), calls=%async_computation.2 | async-start | bytes 1572864 | tf_op jit(solution)/shard_map/all_to_all | solution.py:49
Sparse Core Ops, SparseCore 0:
  64.8 49.2 all-gather.1
where the time goes:
time: 199 us; the launch traced here: 198 us
  blocking collectives  89.5 us (45%)
  waiting for transfers between devices  48.6 us (24%)
  starting transfers between devices  19.4 us (10%)
  between operations  14.1 us (7%)
  matrix products  10.6 us (5%)
  other arithmetic  8.83 us (4%)
  local copies, waits for them, and re-layouts  7.04 us (4%)
    all_to_all x1, blocking collectives, on_device(): lax.all_to_all(send_cot, 'expert', split_axis=0, concat_axis=0, tiled=True)  52 us
    all_to_all x1, blocking collectives, on_device(): lax.all_to_all(send_rows, 'expert', split_axis=0, concat_axis=0, tiled=True)  37.5 us
    all_to_all x1, waiting for transfers between devices, on_device(): lax.all_to_all(expert_out, 'expert', split_axis=0, concat_axis=0, tiled=T...  28 us
    all_to_all x1, waiting for transfers between devices, on_device(): lax.all_to_all(hidden_flat, 'dp', split_axis=1, concat_axis=0, tiled=True)  20.6 us
    all_to_all x1, starting transfers between devices, on_device(): lax.all_to_all(hidden_flat, 'dp', split_axis=1, concat_axis=0, tiled=True)  10.6 us
    all_to_all x1, starting transfers between devices, on_device(): lax.all_to_all(expert_out, 'expert', split_axis=0, concat_axis=0, tiled=T...  8.82 us
    dot_general x1, matrix products, on_device(): jnp.einsum('gsh,gsl->ghl', columns.reshape(groups, slots, share), piece.r...  6.21 us
  transfers between devices with their start and end apart: 3, of which 2 were waited for; matrix products, arithmetic and copies ran while one was open for 5% of the time, Pallas kernels for 0%

commit v1 on v0

v1 whole, which is shorter than its diff:
```python
import functools

import jax
import jax.numpy as jnp
from jax import lax
from jax.experimental import pallas as pl
from jax.experimental.pallas import tpu as pltpu
from jax.sharding import Mesh, PartitionSpec as P

LANES = 128
CORES = 2
VMEM_LIMIT = 48 * 1024 * 1024


def slot_picks(routes_ref, experts, capacity):
    tokens = routes_ref.shape[1]
    named = routes_ref[...] == lax.broadcasted_iota(jnp.int32, (experts, tokens), 0)
    earlier = lax.broadcasted_iota(jnp.int32, (tokens, tokens), 0) < lax.broadcasted_iota(
        jnp.int32, (tokens, tokens), 1
    )
    rank = jnp.dot(
        jnp.where(named, 1.0, 0.0).astype(jnp.bfloat16),
        jnp.where(earlier, 1.0, 0.0).astype(jnp.bfloat16),
        preferred_element_type=jnp.float32,
    )
    return [
        jnp.where(jnp.logical_and(named, rank == float(k)), 1.0, 0.0) for k in range(capacity)
    ]


def pack_kernel(experts, capacity, routes_ref, gates_ref, latent_ref, cot_ref, out_ref, stage):
    chunks = latent_ref.shape[1] // LANES
    block = 2 * capacity * chunks
    for k, pick in enumerate(slot_picks(routes_ref, experts, capacity)):
        gate = jnp.sum(pick * gates_ref[...], axis=1, keepdims=True)
        pick = pick.astype(jnp.bfloat16)
        rows = jnp.dot(pick, latent_ref[...], preferred_element_type=jnp.float32)
        cots = jnp.dot(pick, cot_ref[...], preferred_element_type=jnp.float32) * gate
        for c in range(chunks):
            lanes = slice(c * LANES, (c + 1) * LANES)
            first = 2 * k * chunks + c
            stage[pl.ds(first, experts, stride=block), :] = rows[:, lanes]
            stage[pl.ds(first + chunks, experts, stride=block), :] = cots[:, lanes]
    out_ref[...] = stage[...].astype(jnp.bfloat16)


def unpack(stage, out_ref, at, sources, capacity, parts, part):
    chunks = out_ref.shape[1] // LANES
    block = parts * capacity * chunks
    for k in range(capacity):
        for c in range(chunks):
            out_ref[at + k * sources : at + (k + 1) * sources, c * LANES : (c + 1) * LANES] = stage[
                pl.ds((parts * k + part) * chunks + c, sources, stride=block), :
            ].astype(jnp.bfloat16)


def activation(rows, weight):
    preact = jnp.dot(rows, weight, preferred_element_type=jnp.float32)
    return (jnp.maximum(preact, 0.0) ** 2).astype(jnp.bfloat16)


def expert_kernel(
    sources, capacity, recv_ref, up_ref, down_ref, hidden_ref, cots_ref, out_ref, stage, rows
):
    width = rows.shape[1]
    chunks = width // LANES
    stage[...] = recv_ref[...].astype(jnp.float32)
    unpack(stage, rows, 0, sources, capacity, 2, 0)
    unpack(stage, cots_ref, 0, sources, capacity, 2, 1)
    tile = 2 * LANES

    @pl.loop(0, up_ref.shape[1] // tile)
    def _(j):
        columns = pl.ds(pl.multiple_of(j * tile, tile), tile)
        hidden_ref[:, columns] = activation(rows[...], up_ref[:, columns])

    for j in range(width // tile):
        out = jnp.dot(
            hidden_ref[...],
            down_ref[:, j * tile : (j + 1) * tile],
            preferred_element_type=jnp.float32,
        )
        for k in range(capacity):
            for c in range(tile // LANES):
                first = k * chunks + j * (tile // LANES) + c
                stage[pl.ds(first, sources, stride=capacity * chunks), :] = out[
                    k * sources : (k + 1) * sources, c * LANES : (c + 1) * LANES
                ]
    out_ref[...] = stage[: sources * capacity * chunks, :].astype(jnp.bfloat16)


def grad_kernel(
    sources,
    capacity,
    factor,
    core_ref,
    hidden_ref,
    own_cots_ref,
    other_ref,
    up_ref,
    part_ref,
    stage,
    rows,
    cots,
):
    me = core_ref[0]
    slots = sources * capacity
    stage[...] = other_ref[...].astype(jnp.float32)
    unpack(stage, rows, 0, sources, capacity, 2, 0)
    unpack(stage, cots, slots, sources, capacity, 2, 1)
    cots[:slots, :] = own_cots_ref[...]

    @pl.loop(0, part_ref.shape[0] // (2 * LANES))
    def _(y):
        blocks = [
            pl.ds(pl.multiple_of((CORES * (2 * y + i) + me) * LANES, LANES), LANES)
            for i in range(2)
        ]
        other = activation(
            rows[...], jnp.concatenate([up_ref[:, block] for block in blocks], axis=1)
        )
        own = jnp.concatenate([hidden_ref[:, block] for block in blocks], axis=1)
        product = lax.dot_general(
            jnp.concatenate([own, other], axis=0),
            cots[...],
            (((0,), (0,)), ((), ())),
            preferred_element_type=jnp.float32,
        )
        part_ref[pl.ds(pl.multiple_of(y * 2 * LANES, 2 * LANES), 2 * LANES), :] = (
            factor * product
        ).astype(jnp.bfloat16)


def mix_kernel(experts, capacity, routes_ref, gates_ref, back_ref, out_ref, stage):
    width = out_ref.shape[1]
    chunks = width // LANES
    block = capacity * chunks
    stage[...] = back_ref[...].astype(jnp.float32)
    picks = slot_picks(routes_ref, experts, capacity)
    gates = [jnp.sum(pick * gates_ref[...], axis=1, keepdims=True) for pick in picks]
    picks = jnp.concatenate(picks, axis=0).astype(jnp.bfloat16)
    for c in range(chunks):
        scaled = [
            (gates[k] * stage[pl.ds(k * chunks + c, experts, stride=block), :]).astype(jnp.bfloat16)
            for k in range(capacity)
        ]
        out_ref[:, c * LANES : (c + 1) * LANES] = lax.dot_general(
            picks,
            jnp.concatenate(scaled, axis=0),
            (((0,), (0,)), ((), ())),
            preferred_element_type=jnp.float32,
        ).astype(jnp.bfloat16)


def call(kernel, out_shape, scratch, flops, moved, smem=()):
    def spec(i):
        return pl.BlockSpec(memory_space=pltpu.SMEM if i in smem else pltpu.VMEM)

    def run(*args):
        return pl.pallas_call(
            kernel,
            out_shape=out_shape,
            in_specs=[spec(i) for i in range(len(args))],
            out_specs=jax.tree.map(lambda _: pl.BlockSpec(memory_space=pltpu.VMEM), out_shape),
            scratch_shapes=scratch,
            compiler_params=pltpu.CompilerParams(vmem_limit_bytes=VMEM_LIMIT),
            cost_estimate=pl.CostEstimate(flops=flops, bytes_accessed=moved, transcendentals=0),
        )(*args)

    return run


def on_device(latent, cotangent, routes, gates, up_weight, down_weight):
    experts = lax.axis_size("expert")
    groups = lax.axis_size("y") * lax.axis_size("core")
    tokens, width = latent.shape
    hidden_width = up_weight.shape[2]
    capacity = max(2, 3 * tokens // (2 * experts))
    slots = experts * capacity
    chunks = width // LANES
    factor = 1.0 / (tokens * groups) ** 0.5
    bf16 = functools.partial(jax.ShapeDtypeStruct, dtype=jnp.bfloat16)
    f32 = lambda *shape: pltpu.VMEM(shape, jnp.float32)
    half = lambda *shape: pltpu.VMEM(shape, jnp.bfloat16)
    route_row, gate_row = routes.reshape(1, tokens), gates.reshape(1, tokens)

    sent = call(
        functools.partial(pack_kernel, experts, capacity),
        bf16((2 * slots * chunks, LANES)),
        [f32(2 * slots * chunks, LANES)],
        4 * slots * tokens * width,
        4 * tokens * width + 4 * slots * width,
    )(route_row, gate_row, latent, cotangent)
    received = lax.all_to_all(
        sent.reshape(experts, -1, LANES), "expert", split_axis=0, concat_axis=0, tiled=True
    ).reshape(-1, LANES)
    other = lax.ppermute(received, "core", [(i, CORES - 1 - i) for i in range(CORES)])
    hidden, cots, out = call(
        functools.partial(expert_kernel, experts, capacity),
        (bf16((slots, hidden_width)), bf16((slots, width)), bf16((slots * chunks, LANES))),
        [f32(2 * slots * chunks, LANES), half(slots, width)],
        4 * slots * width * hidden_width,
        4 * width * hidden_width + 8 * slots * width + 2 * slots * hidden_width,
    )(received, up_weight[0], down_weight[0])
    core = lax.axis_index("core").astype(jnp.int32).reshape(1)
    share = hidden_width // CORES
    partial = call(
        functools.partial(grad_kernel, experts, capacity, factor),
        bf16((share, width)),
        [
            f32(2 * slots * chunks, LANES),
            half(slots, width),
            half(CORES * slots, width),
        ],
        3 * slots * width * hidden_width,
        2 * width * hidden_width + 6 * slots * width + 2 * share * width,
        smem=(0,),
    )(core, hidden, cots, other, up_weight[0])
    down_grad = lax.psum_scatter(partial, "y", scatter_dimension=0, tiled=True)
    returned = lax.all_to_all(
        out.reshape(experts, -1, LANES), "expert", split_axis=0, concat_axis=0, tiled=True
    ).reshape(-1, LANES)
    mixed = call(
        functools.partial(mix_kernel, experts, capacity),
        bf16((tokens, width)),
        [f32(slots * chunks, LANES)],
        2 * slots * tokens * width,
        2 * slots * width + 2 * tokens * width,
    )(route_row, gate_row, returned)
    return mixed, down_grad[None]


def solution(mesh):
    experts, groups = mesh.devices.shape
    split = Mesh(mesh.devices.reshape(experts, groups // CORES, CORES), ("expert", "y", "core"))
    rows = P(("expert", "y", "core"), None)
    weights = P("expert", None, None)
    return jax.shard_map(
        on_device,
        mesh=split,
        in_specs=(rows, rows, rows, rows, weights, weights),
        out_specs=(rows, P("expert", ("y", "core"), None)),
        check_vma=False,
    )
```

time: 199 us -> 142 us (0.71)
  the two profiles are of different devices: /device:TPU:1 before, /device:TPU:6 now
where the time goes in v1:
time: 142 us
  blocking collectives  98.4 us (69%)
  Pallas kernels  17.2 us (12%)
  between operations  14.1 us (10%)
  waiting for transfers between devices  7.27 us (5%)
  local copies, waits for them, and re-layouts  3.21 us (2%)
  starting transfers between devices  1.95 us (1%)
    all_to_all x1, blocking collectives, on_device(): lax.all_to_all(sent.reshape(experts, -1, LANES), 'expert', split_axis=0,...  65 us
    all_to_all x1, blocking collectives, on_device(): lax.all_to_all(out.reshape(experts, -1, LANES), 'expert', split_axis=0, c...  33.4 us
    pallas_call x4, Pallas kernels, run(): pl.pallas_call(kernel, out_shape=out_shape, in_specs=[spec(i) for i in ra...  17.2 us
    reduce_scatter x1, waiting for transfers between devices, on_device(): down_grad = lax.psum_scatter(partial, 'y', scatter_dimension=0, tiled=True)  7.25 us
    unnamed x12, local copies, waits for them, and re-layouts  3.21 us
  transfers between devices with their start and end apart: 2, of which 1 were waited for; matrix products, arithmetic and copies ran while one was open for 0% of the time, Pallas kernels for 6%

profile of v1, /device:TPU:6, one launch (start us, length us, event | category | flops | bytes accessed | tf_op | source)
XLA Modules:
  0.0 142.1 jit_solution(11009918582007278623)
XLA Ops:
  7.2 0.0 reduce-scatter.2.cloned.1.call-start
  7.2 0.0 copy-start
  7.2 0.9 copy-done
  8.2 0.0 copy-start.1
  8.2 0.9 copy-done.1
  9.1 0.0 copy-start.2
  9.1 0.7 copy-done.2
  9.8 0.0 copy-start.4
  9.8 0.7 copy-done.4
  10.4 0.9 shard_map.77
  11.3 65.0 %all_to_all.10 = bf16[64,48,128]{2,1,0:T(8,128)(2,1)S(1)} all-to-all(bf16[64,48,128]{2,1,0:T(8,128)(2,1)S(1)} %bitcast.12), channel_id=1, replica_groups=mesh['expert'=64,'y'=8,'core'=2] {'expert'}, dimensions={0} | all-to-all | bytes 1572864 | tf_op jit(solution)/shard_map/all_to_all | solution.py:194
  76.3 1.9 %collective-permute-start = (bf16[3072,128]{1,0:T(8,128)(2,1)S(1)}, bf16[3072,128]{1,0:T(8,128)(2,1)S(1)}, u32[]{:S(2)}, u32[]{:S(2)}) collective-permute-start(bf16[3072,128]{1,0:T(8,128)(2,1)S(1)} %bitcast.10), channel_id=1, source_target_pairs={{0,1},{1,0},{2,3},{3,2},{4,5},{5,4},{6,7},{7,6},{8,9},{9,8},{10,11... | collective-permute-start | bytes 2359304 | tf_op jit(solution)/shard_map/ppermute | solution.py:197
  78.2 7.4 %shard_map.78 = (bf16[192,2048]{1,0:T(8,128)(2,1)S(1)}, bf16[192,1024]{1,0:T(8,128)(2,1)S(1)}, bf16[1536,128]{1,0:T(8,128)(2,1)S(1)}) custom-call(bf16[3072,128]{1,0:T(8,128)(2,1)S(1)} %bitcast.11, bf16[1024,2048]{1,0:T(8,128)(2,1)} %bitcast.19, bf16[2048,1024]{1,0:T(8,128)(2,1)} %bitcast.21), custom_call_target="tpu_custom_call" | custom-call | flops 1610612736 | bytes 10747904 | tf_op jit(solution)/shard_map/pallas_call | solution.py:160
  85.6 0.0 collective-permute-done.other_ref
  85.6 0.0 copy-start.3
  85.7 0.0 copy-start.5
  85.7 7.6 %shard_map.80 = bf16[1024,1024]{1,0:T(8,128)(2,1)} custom-call(s32[1]{0:T(128)} %bitcast.8.core_ref, bf16[192,2048]{1,0:T(8,128)(2,1)S(1)} %get-tuple-element.6.hidden_ref, bf16[192,1024]{1,0:T(8,128)(2,1)S(1)} %get-tuple-element.7.own_cots_ref, bf16[3072,128]{1,0:T(8,128)(2,1)S(1)} %collective-permute-done.other_ref, bf16[1024,2048]{1,0:T(8,128)(2,1)} %bitcast.20), custom_call_target="tpu_custom_call" | custom-call | flops 1207959552 | bytes 7471104 | tf_op jit(solution)/shard_map/pallas_call | solution.py:160
  93.3 0.0 reduce-scatter.2.cloned.1.call-update
  93.3 33.4 %all_to_all.11 = bf16[64,24,128]{2,1,0:T(8,128)(2,1)S(1)} all-to-all(bf16[64,24,128]{2,1,0:T(8,128)(2,1)S(1)} %bitcast.14), channel_id=1, replica_groups=mesh['expert'=64,'y'=8,'core'=2] {'expert'}, dimensions={0} | all-to-all | bytes 786432 | tf_op jit(solution)/shard_map/all_to_all | solution.py:220
  126.8 0.0 copy-done.3
  126.8 0.0 copy-done.5
  126.8 1.3 shard_map.79
  128.0 7.3 %reduce-scatter.2.cloned.1.call-done = bf16[128,1024]{1,0:T(8,128)(2,1)} async-done(((bf16[1024,1024]{1,0:T(8,128)(2,1)}), bf16[128,1024]{1,0:T(8,128)(2,1)}) %reduce-scatter.2.cloned.1.call-update) | async-done | bytes 262160 | tf_op jit(solution)/shard_map/reduce_scatter | solution.py:219
Async XLA Ops:
  7.2 128.1 %reduce-scatter.2.cloned.1.call-start = ((), (), s32[]{:S(2)}) async-start(), calls=%async_computation.3 | async-start | bytes 2359296 | tf_op jit(solution)/shard_map/reduce_scatter | solution.py:219
  7.2 1.0 copy-start
  8.2 0.9 copy-start.1
  9.1 0.7 copy-start.2
  9.8 0.7 copy-start.4
  76.3 9.3 %collective-permute-start = (bf16[3072,128]{1,0:T(8,128)(2,1)S(1)}, bf16[3072,128]{1,0:T(8,128)(2,1)S(1)}, u32[]{:S(2)}, u32[]{:S(2)}) collective-permute-start(bf16[3072,128]{1,0:T(8,128)(2,1)S(1)} %bitcast.10), channel_id=1, source_target_pairs={{0,1},{1,0},{2,3},{3,2},{4,5},{5,4},{6,7},{7,6},{8,9},{9,8},{10,11... | collective-permute-start | bytes 2359304 | tf_op jit(solution)/shard_map/ppermute | solution.py:197
  85.6 41.1 %copy-start.3 = (s32[128,1]{0,1:T(1,128)S(1)}, s32[128,1]{0,1:T(1,128)}, u32[]{:S(2)}) copy-start(s32[128,1]{0,1:T(1,128)} %param.8) | copy-start | bytes 1540
  85.7 41.1 %copy-start.5 = (f32[128,1]{0,1:T(1,128)S(1)}, f32[128,1]{0,1:T(1,128)}, u32[]{:S(2)}) copy-start(f32[128,1]{0,1:T(1,128)} %param.9) | copy-start | bytes 1540
Sparse Core Ops, SparseCore 0:
  93.5 41.7 reduce-scatter.1

commit v2 on v1

--- a/solution.py
+++ b/solution.py
@@ -28,19 +28,33 @@
     ]
 
 
-def pack_kernel(experts, capacity, routes_ref, gates_ref, latent_ref, cot_ref, out_ref, stage):
-    chunks = latent_ref.shape[1] // LANES
+def pack_kernel(
+    experts, capacity, routes_hbm, gates_hbm, latent_hbm, cot_hbm, out_ref, stage, routes, gates, latent, cot, sems
+):
+    copies = [
+        pltpu.make_async_copy(source, target, sems.at[i])
+        for i, (source, target) in enumerate(
+            ((routes_hbm, routes), (gates_hbm, gates), (latent_hbm, latent), (cot_hbm, cot))
+        )
+    ]
+    for copy in copies:
+        copy.start()
+    chunks = latent.shape[1] // LANES
     block = 2 * capacity * chunks
-    for k, pick in enumerate(slot_picks(routes_ref, experts, capacity)):
-        gate = jnp.sum(pick * gates_ref[...], axis=1, keepdims=True)
-        pick = pick.astype(jnp.bfloat16)
-        rows = jnp.dot(pick, latent_ref[...], preferred_element_type=jnp.float32)
-        cots = jnp.dot(pick, cot_ref[...], preferred_element_type=jnp.float32) * gate
-        for c in range(chunks):
-            lanes = slice(c * LANES, (c + 1) * LANES)
-            first = 2 * k * chunks + c
-            stage[pl.ds(first, experts, stride=block), :] = rows[:, lanes]
-            stage[pl.ds(first + chunks, experts, stride=block), :] = cots[:, lanes]
+    copies[0].wait()
+    copies[1].wait()
+    picks = slot_picks(routes, experts, capacity)
+    for part, source in enumerate((latent, cot)):
+        copies[2 + part].wait()
+        for k, pick in enumerate(picks):
+            rows = jnp.dot(
+                pick.astype(jnp.bfloat16), source[...], preferred_element_type=jnp.float32
+            )
+            if part == 1:
+                rows = rows * jnp.sum(pick * gates[...], axis=1, keepdims=True)
+            for c in range(chunks):
+                first = (2 * k + part) * chunks + c
+                stage[pl.ds(first, experts, stride=block), :] = rows[:, c * LANES : (c + 1) * LANES]
     out_ref[...] = stage[...].astype(jnp.bfloat16)
 
 
@@ -59,34 +73,27 @@
     return (jnp.maximum(preact, 0.0) ** 2).astype(jnp.bfloat16)
 
 
-def expert_kernel(
-    sources, capacity, recv_ref, up_ref, down_ref, hidden_ref, cots_ref, out_ref, stage, rows
+def hidden_kernel(
+    sources, capacity, recv_ref, up_hbm, hidden_ref, cots_ref, stage, rows, up, sems
 ):
-    width = rows.shape[1]
-    chunks = width // LANES
+    tile = 2 * LANES
+    tiles = up.shape[1] // tile
+
+    def fetch(j):
+        columns = pl.ds(pl.multiple_of(j * tile, tile), tile)
+        return pltpu.make_async_copy(up_hbm.at[:, columns], up.at[:, columns], sems.at[j])
+
+    for j in range(tiles):
+        fetch(j).start()
     stage[...] = recv_ref[...].astype(jnp.float32)
     unpack(stage, rows, 0, sources, capacity, 2, 0)
     unpack(stage, cots_ref, 0, sources, capacity, 2, 1)
-    tile = 2 * LANES
-
-    @pl.loop(0, up_ref.shape[1] // tile)
+
+    @pl.loop(0, tiles)
     def _(j):
+        fetch(j).wait()
         columns = pl.ds(pl.multiple_of(j * tile, tile), tile)
-        hidden_ref[:, columns] = activation(rows[...], up_ref[:, columns])
-
-    for j in range(width // tile):
-        out = jnp.dot(
-            hidden_ref[...],
-            down_ref[:, j * tile : (j + 1) * tile],
-            preferred_element_type=jnp.float32,
-        )
-        for k in range(capacity):
-            for c in range(tile // LANES):
-                first = k * chunks + j * (tile // LANES) + c
-                stage[pl.ds(first, sources, stride=capacity * chunks), :] = out[
-                    k * sources : (k + 1) * sources, c * LANES : (c + 1) * LANES
-                ]
-    out_ref[...] = stage[: sources * capacity * chunks, :].astype(jnp.bfloat16)
+        hidden_ref[:, columns] = activation(rows[...], up[:, columns])
 
 
 def grad_kernel(
@@ -97,38 +104,87 @@
     hidden_ref,
     own_cots_ref,
     other_ref,
-    up_ref,
-    part_ref,
+    up_hbm,
+    part_hbm,
     stage,
     rows,
     cots,
+    up,
+    part,
+    sems,
+    out_sems,
 ):
     me = core_ref[0]
     slots = sources * capacity
+    blocks = part.shape[0] // LANES
+
+    def source_columns(y):
+        return pl.ds(pl.multiple_of((CORES * y + me) * LANES, LANES), LANES)
+
+    def fetch(y):
+        return pltpu.make_async_copy(
+            up_hbm.at[:, source_columns(y)],
+            up.at[:, pl.ds(pl.multiple_of(y * LANES, LANES), LANES)],
+            sems.at[y],
+        )
+
+    def flush(j):
+        at = pl.ds(pl.multiple_of(j * 2 * LANES, 2 * LANES), 2 * LANES)
+        return pltpu.make_async_copy(part.at[at, :], part_hbm.at[at, :], out_sems.at[j])
+
+    for y in range(blocks):
+        fetch(y).start()
     stage[...] = other_ref[...].astype(jnp.float32)
     unpack(stage, rows, 0, sources, capacity, 2, 0)
     unpack(stage, cots, slots, sources, capacity, 2, 1)
     cots[:slots, :] = own_cots_ref[...]
 
-    @pl.loop(0, part_ref.shape[0] // (2 * LANES))
-    def _(y):
-        blocks = [
-            pl.ds(pl.multiple_of((CORES * (2 * y + i) + me) * LANES, LANES), LANES)
-            for i in range(2)
-        ]
-        other = activation(
-            rows[...], jnp.concatenate([up_ref[:, block] for block in blocks], axis=1)
-        )
-        own = jnp.concatenate([hidden_ref[:, block] for block in blocks], axis=1)
+    @pl.loop(0, blocks // 2)
+    def _(j):
+        fetch(2 * j).wait()
+        fetch(2 * j + 1).wait()
+        at = pl.ds(pl.multiple_of(j * 2 * LANES, 2 * LANES), 2 * LANES)
+        other = activation(rows[...], up[:, at])
+        own = jnp.concatenate([hidden_ref[:, source_columns(2 * j + i)] for i in range(2)], axis=1)
         product = lax.dot_general(
             jnp.concatenate([own, other], axis=0),
             cots[...],
             (((0,), (0,)), ((), ())),
             preferred_element_type=jnp.float32,
         )
-        part_ref[pl.ds(pl.multiple_of(y * 2 * LANES, 2 * LANES), 2 * LANES), :] = (
-            factor * product
-        ).astype(jnp.bfloat16)
+        part[at, :] = (factor * product).astype(jnp.bfloat16)
+        flush(j).start()
+
+    for j in range(blocks // 2):
+        flush(j).wait()
+
+
+def down_kernel(sources, capacity, hidden_ref, down_hbm, out_ref, stage, down, sems):
+    width = down.shape[1]
+    chunks = width // LANES
+    tile = 2 * LANES
+    copies = [
+        pltpu.make_async_copy(
+            down_hbm.at[:, pl.ds(j * tile, tile)], down.at[:, pl.ds(j * tile, tile)], sems.at[j]
+        )
+        for j in range(width // tile)
+    ]
+    for copy in copies:
+        copy.start()
+    for j, copy in enumerate(copies):
+        copy.wait()
+        out = jnp.dot(
+            hidden_ref[...],
+            down[:, j * tile : (j + 1) * tile],
+            preferred_element_type=jnp.float32,
+        )
+        for k in range(capacity):
+            for c in range(tile // LANES):
+                first = k * chunks + j * (tile // LANES) + c
+                stage[pl.ds(first, sources, stride=capacity * chunks), :] = out[
+                    k * sources : (k + 1) * sources, c * LANES : (c + 1) * LANES
+                ]
+    out_ref[...] = stage[...].astype(jnp.bfloat16)
 
 
 def mix_kernel(experts, capacity, routes_ref, gates_ref, back_ref, out_ref, stage):
@@ -152,16 +208,23 @@
         ).astype(jnp.bfloat16)
 
 
-def call(kernel, out_shape, scratch, flops, moved, smem=()):
+def call(kernel, out_shape, scratch, flops, moved, smem=(), hbm=(), out_hbm=False):
     def spec(i):
-        return pl.BlockSpec(memory_space=pltpu.SMEM if i in smem else pltpu.VMEM)
+        space = pltpu.SMEM if i in smem else pltpu.HBM if i in hbm else pltpu.VMEM
+        return pl.BlockSpec(memory_space=space)
+
+    out_space = pltpu.HBM if out_hbm else pltpu.VMEM
 
     def run(*args):
+        args = [
+            pltpu.with_memory_space_constraint(a, pltpu.HBM) if i in hbm else a
+            for i, a in enumerate(args)
+        ]
         return pl.pallas_call(
             kernel,
             out_shape=out_shape,
             in_specs=[spec(i) for i in range(len(args))],
-            out_specs=jax.tree.map(lambda _: pl.BlockSpec(memory_space=pltpu.VMEM), out_shape),
+            out_specs=jax.tree.map(lambda _: pl.BlockSpec(memory_space=out_space), out_shape),
             scratch_shapes=scratch,
             compiler_params=pltpu.CompilerParams(vmem_limit_bytes=VMEM_LIMIT),
             cost_estimate=pl.CostEstimate(flops=flops, bytes_accessed=moved, transcendentals=0),
@@ -184,24 +247,39 @@
     half = lambda *shape: pltpu.VMEM(shape, jnp.bfloat16)
     route_row, gate_row = routes.reshape(1, tokens), gates.reshape(1, tokens)
 
+    sems = lambda n: pltpu.SemaphoreType.DMA((n,))
     sent = call(
         functools.partial(pack_kernel, experts, capacity),
         bf16((2 * slots * chunks, LANES)),
-        [f32(2 * slots * chunks, LANES)],
+        [
+            f32(2 * slots * chunks, LANES),
+            pltpu.VMEM((1, tokens), jnp.int32),
+            f32(1, tokens),
+            half(tokens, width),
+            half(tokens, width),
+            sems(4),
+        ],
         4 * slots * tokens * width,
         4 * tokens * width + 4 * slots * width,
+        hbm=(0, 1, 2, 3),
     )(route_row, gate_row, latent, cotangent)
     received = lax.all_to_all(
         sent.reshape(experts, -1, LANES), "expert", split_axis=0, concat_axis=0, tiled=True
     ).reshape(-1, LANES)
     other = lax.ppermute(received, "core", [(i, CORES - 1 - i) for i in range(CORES)])
-    hidden, cots, out = call(
-        functools.partial(expert_kernel, experts, capacity),
-        (bf16((slots, hidden_width)), bf16((slots, width)), bf16((slots * chunks, LANES))),
-        [f32(2 * slots * chunks, LANES), half(slots, width)],
-        4 * slots * width * hidden_width,
-        4 * width * hidden_width + 8 * slots * width + 2 * slots * hidden_width,
-    )(received, up_weight[0], down_weight[0])
+    hidden, cots = call(
+        functools.partial(hidden_kernel, experts, capacity),
+        (bf16((slots, hidden_width)), bf16((slots, width))),
+        [
+            f32(2 * slots * chunks, LANES),
+            half(slots, width),
+            half(width, hidden_width),
+            sems(hidden_width // (2 * LANES)),
+        ],
+        2 * slots * width * hidden_width,
+        2 * width * hidden_width + 6 * slots * width + 2 * slots * hidden_width,
+        hbm=(1,),
+    )(received, up_weight[0])
     core = lax.axis_index("core").astype(jnp.int32).reshape(1)
     share = hidden_width // CORES
     partial = call(
@@ -211,12 +289,31 @@
             f32(2 * slots * chunks, LANES),
             half(slots, width),
             half(CORES * slots, width),
+            half(width, share),
+            half(share, width),
+            sems(share // LANES),
+            sems(share // (2 * LANES)),
         ],
         3 * slots * width * hidden_width,
-        2 * width * hidden_width + 6 * slots * width + 2 * share * width,
+        width * hidden_width + 6 * slots * width + 2 * share * width,
         smem=(0,),
+        hbm=(4,),
+        out_hbm=True,
     )(core, hidden, cots, other, up_weight[0])
     down_grad = lax.psum_scatter(partial, "y", scatter_dimension=0, tiled=True)
+    hidden, partial = lax.optimization_barrier((hidden, partial))
+    out = call(
+        functools.partial(down_kernel, experts, capacity),
+        bf16((slots * chunks, LANES)),
+        [
+            f32(slots * chunks, LANES),
+            half(hidden_width, width),
+            sems(width // (2 * LANES)),
+        ],
+        2 * slots * width * hidden_width,
+        2 * width * hidden_width + 2 * slots * width + 2 * slots * hidden_width,
+        hbm=(1,),
+    )(hidden, down_weight[0])
     returned = lax.all_to_all(
         out.reshape(experts, -1, LANES), "expert", split_axis=0, concat_axis=0, tiled=True
     ).reshape(-1, LANES)

time: 142 us -> 134 us (0.944)
  waiting for transfers between devices: 7.27 us -> 3.75 us
  local copies, waits for them, and re-layouts: 3.21 us -> 0.01 us
  Pallas kernels: 17.2 us -> 15.4 us
    reduce_scatter x1, waiting for transfers between devices: 7.25 us -> 3.73 us  [on_device(): down_grad = lax.psum_scatter(partial, 'y', scatter_dimension=0, tiled=True)]
    unnamed x12 -> x4, local copies, waits for them, and re-layouts: 3.21 us -> 0.01 us
    pallas_call x4 -> x5, Pallas kernels: 17.2 us -> 15.4 us  [run(): pl.pallas_call(kernel, out_shape=out_shape, in_specs=[spec(i) for i in ra...]
where the time goes in v2:
time: 134 us
  blocking collectives  98.4 us (73%)
  Pallas kernels  15.4 us (11%)
  between operations  14.1 us (11%)
  waiting for transfers between devices  3.75 us (3%)
  starting transfers between devices  1.95 us (1%)
    all_to_all x1, blocking collectives, on_device(): lax.all_to_all(sent.reshape(experts, -1, LANES), 'expert', split_axis=0,...  65 us
    all_to_all x1, blocking collectives, on_device(): lax.all_to_all(out.reshape(experts, -1, LANES), 'expert', split_axis=0, c...  33.4 us
    pallas_call x5, Pallas kernels, run(): pl.pallas_call(kernel, out_shape=out_shape, in_specs=[spec(i) for i in ra...  15.4 us
    reduce_scatter x1, waiting for transfers between devices, on_device(): down_grad = lax.psum_scatter(partial, 'y', scatter_dimension=0, tiled=True)  3.73 us
  transfers between devices with their start and end apart: 2, of which 1 were waited for; matrix products, arithmetic and copies ran while one was open for 0% of the time, Pallas kernels for 6%

profile of v2, /device:TPU:6, one launch (start us, length us, event | category | flops | bytes accessed | tf_op | source)
XLA Modules:
  0.0 133.7 jit_solution(14308486669258158219)
XLA Ops:
  7.2 0.0 reduce-scatter.2.cloned.1.call-start
  7.2 1.8 %shard_map.77 = bf16[3072,128]{1,0:T(8,128)(2,1)S(1)} custom-call(s32[1,128]{1,0:T(1,128)} %bitcast.15, f32[1,128]{1,0:T(1,128)} %bitcast.17, bf16[128,1024]{1,0:T(8,128)(2,1)} %latent_hbm.1, bf16[128,1024]{1,0:T(8,128)(2,1)} %cot_hbm.1), custom_call_target="tpu_custom_call" | custom-call | flops 100663296 | bytes 1310720 | tf_op jit(solution)/shard_map/pallas_call | solution.py:223
  9.1 65.0 %all_to_all.10 = bf16[64,48,128]{2,1,0:T(8,128)(2,1)S(1)} all-to-all(bf16[64,48,128]{2,1,0:T(8,128)(2,1)S(1)} %bitcast.12), channel_id=1, replica_groups=mesh['expert'=64,'y'=8,'core'=2] {'expert'}, dimensions={0} | all-to-all | bytes 1572864 | tf_op jit(solution)/shard_map/all_to_all | solution.py:266
  74.1 1.9 %collective-permute-start = (bf16[3072,128]{1,0:T(8,128)(2,1)S(1)}, bf16[3072,128]{1,0:T(8,128)(2,1)S(1)}, u32[]{:S(2)}, u32[]{:S(2)}) collective-permute-start(bf16[3072,128]{1,0:T(8,128)(2,1)S(1)} %bitcast.10), channel_id=1, source_target_pairs={{0,1},{1,0},{2,3},{3,2},{4,5},{5,4},{6,7},{7,6},{8,9},{9,8},{10,11... | collective-permute-start | bytes 2359304 | tf_op jit(solution)/shard_map/ppermute | solution.py:269
  76.0 3.4 %shard_map.78 = (bf16[192,2048]{1,0:T(8,128)(2,1)S(1)}, bf16[192,1024]{1,0:T(8,128)(2,1)S(1)}) custom-call(bf16[3072,128]{1,0:T(8,128)(2,1)S(1)} %bitcast.11, bf16[1024,2048]{1,0:T(8,128)(2,1)} %bitcast.19), custom_call_target="tpu_custom_call" | custom-call | flops 805306368 | bytes 6160384 | tf_op jit(solution)/shard_map/pallas_call | solution.py:223
  79.4 0.0 collective-permute-done.other_ref
  79.5 5.4 %shard_map.79 = bf16[1024,1024]{1,0:T(8,128)(2,1)} custom-call(s32[1]{0:T(128)} %bitcast.5.core_ref, bf16[192,2048]{1,0:T(8,128)(2,1)S(1)} %get-tuple-element.7.hidden_ref, bf16[192,1024]{1,0:T(8,128)(2,1)S(1)} %get-tuple-element.6.own_cots_ref, bf16[3072,128]{1,0:T(8,128)(2,1)S(1)} %collective-permute-done.other_ref, bf16[1024,2048]{1,0:T(8,128)(2,1)} %bitcast.20), custom_call_target="tpu_custom_call" | custom-call | flops 1207959552 | bytes 5373952 | tf_op jit(solution)/shard_map/pallas_call | solution.py:223
  84.8 0.0 copy-start
  84.8 0.0 copy-start.1
  84.9 0.0 reduce-scatter.2.cloned.1.call-update
  84.9 3.5 %shard_map.80 = bf16[1536,128]{1,0:T(8,128)(2,1)S(1)} custom-call(bf16[192,2048]{1,0:T(8,128)(2,1)S(1)} %get-tuple-element.7.hidden_ref, bf16[2048,1024]{1,0:T(8,128)(2,1)} %bitcast.21), custom_call_target="tpu_custom_call" | custom-call | flops 805306368 | bytes 5373952 | tf_op jit(solution)/shard_map/pallas_call | solution.py:223
  88.4 33.4 %all_to_all.11 = bf16[64,24,128]{2,1,0:T(8,128)(2,1)S(1)} all-to-all(bf16[64,24,128]{2,1,0:T(8,128)(2,1)S(1)} %bitcast.14), channel_id=1, replica_groups=mesh['expert'=64,'y'=8,'core'=2] {'expert'}, dimensions={0} | all-to-all | bytes 786432 | tf_op jit(solution)/shard_map/all_to_all | solution.py:317
  121.8 0.0 copy-done
  121.8 0.0 copy-done.1
  121.8 1.3 shard_map.81
  123.1 3.7 %reduce-scatter.2.cloned.1.call-done = bf16[128,1024]{1,0:T(8,128)(2,1)} async-done(((bf16[1024,1024]{1,0:T(8,128)(2,1)}), bf16[128,1024]{1,0:T(8,128)(2,1)}) %reduce-scatter.2.cloned.1.call-update) | async-done | bytes 262160 | tf_op jit(solution)/shard_map/reduce_scatter | solution.py:303
Async XLA Ops:
  7.2 119.6 %reduce-scatter.2.cloned.1.call-start = ((), (), s32[]{:S(2)}) async-start(), calls=%async_computation.3 | async-start | bytes 2359296 | tf_op jit(solution)/shard_map/reduce_scatter | solution.py:303
  74.1 5.4 %collective-permute-start = (bf16[3072,128]{1,0:T(8,128)(2,1)S(1)}, bf16[3072,128]{1,0:T(8,128)(2,1)S(1)}, u32[]{:S(2)}, u32[]{:S(2)}) collective-permute-start(bf16[3072,128]{1,0:T(8,128)(2,1)S(1)} %bitcast.10), channel_id=1, source_target_pairs={{0,1},{1,0},{2,3},{3,2},{4,5},{5,4},{6,7},{7,6},{8,9},{9,8},{10,11... | collective-permute-start | bytes 2359304 | tf_op jit(solution)/shard_map/ppermute | solution.py:269
  84.8 37.0 %copy-start = (s32[128,1]{0,1:T(1,128)S(1)}, s32[128,1]{0,1:T(1,128)}, u32[]{:S(2)}) copy-start(s32[128,1]{0,1:T(1,128)} %param.8) | copy-start | bytes 1540
  84.8 37.0 %copy-start.1 = (f32[128,1]{0,1:T(1,128)S(1)}, f32[128,1]{0,1:T(1,128)}, u32[]{:S(2)}) copy-start(f32[128,1]{0,1:T(1,128)} %param.9) | copy-start | bytes 1540
Sparse Core Ops, SparseCore 0:
  85.0 41.7 reduce-scatter.1

commit v3 on v2

--- a/solution.py
+++ b/solution.py
@@ -9,7 +9,7 @@
 
 LANES = 128
 CORES = 2
-VMEM_LIMIT = 48 * 1024 * 1024
+VMEM_LIMIT = 24 * 1024 * 1024
 
 
 def slot_picks(routes_ref, experts, capacity):
@@ -74,92 +74,81 @@
 
 
 def hidden_kernel(
-    sources, capacity, recv_ref, up_hbm, hidden_ref, cots_ref, stage, rows, up, sems
+    sources, capacity, recv_ref, up_hbm, hidden_ref, cots_ref, up_ref, stage, rows, sems
 ):
-    tile = 2 * LANES
-    tiles = up.shape[1] // tile
-
-    def fetch(j):
-        columns = pl.ds(pl.multiple_of(j * tile, tile), tile)
-        return pltpu.make_async_copy(up_hbm.at[:, columns], up.at[:, columns], sems.at[j])
-
-    for j in range(tiles):
-        fetch(j).start()
+    tile = 4 * LANES
+    columns = [pl.ds(j * tile, tile) for j in range(up_ref.shape[1] // tile)]
+    copies = [
+        pltpu.make_async_copy(up_hbm.at[:, at], up_ref.at[:, at], sems.at[j])
+        for j, at in enumerate(columns)
+    ]
+    for copy in copies:
+        copy.start()
     stage[...] = recv_ref[...].astype(jnp.float32)
     unpack(stage, rows, 0, sources, capacity, 2, 0)
     unpack(stage, cots_ref, 0, sources, capacity, 2, 1)
-
-    @pl.loop(0, tiles)
-    def _(j):
-        fetch(j).wait()
-        columns = pl.ds(pl.multiple_of(j * tile, tile), tile)
-        hidden_ref[:, columns] = activation(rows[...], up[:, columns])
-
-
-def grad_kernel(
+    for copy, at in zip(copies, columns):
+        copy.wait()
+        hidden_ref[:, at] = activation(rows[...], up_ref[:, at])
+
+
+def block_product(factor, place_ref, offset, hidden_ref, rows_ref, cots_ref, up_ref):
+    y = lax.rem(place_ref[0] + offset, place_ref[2])
+    at = pl.ds(pl.multiple_of((CORES * y + place_ref[1]) * LANES, LANES), LANES)
+    other = activation(rows_ref[...], up_ref[:, at])
+    product = lax.dot_general(
+        jnp.concatenate([hidden_ref[:, at], other], axis=0),
+        cots_ref[...],
+        (((0,), (0,)), ((), ())),
+        preferred_element_type=jnp.float32,
+    )
+    return (factor * product).astype(jnp.bfloat16)
+
+
+def first_grad_kernel(
     sources,
     capacity,
     factor,
-    core_ref,
+    offsets,
+    place_ref,
     hidden_ref,
     own_cots_ref,
     other_ref,
-    up_hbm,
-    part_hbm,
+    up_ref,
+    up_block_ref,
+    down_block_ref,
+    rows_ref,
+    cots_ref,
     stage,
-    rows,
-    cots,
-    up,
-    part,
+):
+    slots = sources * capacity
+    stage[...] = other_ref[...].astype(jnp.float32)
+    unpack(stage, rows_ref, 0, sources, capacity, 2, 0)
+    unpack(stage, cots_ref, slots, sources, capacity, 2, 1)
+    cots_ref[:slots, :] = own_cots_ref[...]
+    for out_ref, offset in zip((up_block_ref, down_block_ref), offsets):
+        out_ref[...] = block_product(
+            factor, place_ref, offset, hidden_ref, rows_ref, cots_ref, up_ref
+        )
+
+
+def rest_kernel(
+    sources,
+    capacity,
+    factor,
+    offsets,
+    place_ref,
+    hidden_ref,
+    rows_ref,
+    cots_ref,
+    up_ref,
+    down_hbm,
+    part_ref,
+    out_ref,
+    stage,
+    down,
     sems,
-    out_sems,
 ):
-    me = core_ref[0]
-    slots = sources * capacity
-    blocks = part.shape[0] // LANES
-
-    def source_columns(y):
-        return pl.ds(pl.multiple_of((CORES * y + me) * LANES, LANES), LANES)
-
-    def fetch(y):
-        return pltpu.make_async_copy(
-            up_hbm.at[:, source_columns(y)],
-            up.at[:, pl.ds(pl.multiple_of(y * LANES, LANES), LANES)],
-            sems.at[y],
-        )
-
-    def flush(j):
-        at = pl.ds(pl.multiple_of(j * 2 * LANES, 2 * LANES), 2 * LANES)
-        return pltpu.make_async_copy(part.at[at, :], part_hbm.at[at, :], out_sems.at[j])
-
-    for y in range(blocks):
-        fetch(y).start()
-    stage[...] = other_ref[...].astype(jnp.float32)
-    unpack(stage, rows, 0, sources, capacity, 2, 0)
-    unpack(stage, cots, slots, sources, capacity, 2, 1)
-    cots[:slots, :] = own_cots_ref[...]
-
-    @pl.loop(0, blocks // 2)
-    def _(j):
-        fetch(2 * j).wait()
-        fetch(2 * j + 1).wait()
-        at = pl.ds(pl.multiple_of(j * 2 * LANES, 2 * LANES), 2 * LANES)
-        other = activation(rows[...], up[:, at])
-        own = jnp.concatenate([hidden_ref[:, source_columns(2 * j + i)] for i in range(2)], axis=1)
-        product = lax.dot_general(
-            jnp.concatenate([own, other], axis=0),
-            cots[...],
-            (((0,), (0,)), ((), ())),
-            preferred_element_type=jnp.float32,
-        )
-        part[at, :] = (factor * product).astype(jnp.bfloat16)
-        flush(j).start()
-
-    for j in range(blocks // 2):
-        flush(j).wait()
-
-
-def down_kernel(sources, capacity, hidden_ref, down_hbm, out_ref, stage, down, sems):
     width = down.shape[1]
     chunks = width // LANES
     tile = 2 * LANES
@@ -171,6 +160,10 @@
     ]
     for copy in copies:
         copy.start()
+    for i, offset in enumerate(offsets):
+        part_ref[i] = block_product(
+            factor, place_ref, offset, hidden_ref, rows_ref, cots_ref, up_ref
+        )
     for j, copy in enumerate(copies):
         copy.wait()
         out = jnp.dot(
@@ -267,53 +260,65 @@
         sent.reshape(experts, -1, LANES), "expert", split_axis=0, concat_axis=0, tiled=True
     ).reshape(-1, LANES)
     other = lax.ppermute(received, "core", [(i, CORES - 1 - i) for i in range(CORES)])
-    hidden, cots = call(
+    hidden, cots, up = call(
         functools.partial(hidden_kernel, experts, capacity),
-        (bf16((slots, hidden_width)), bf16((slots, width))),
+        (
+            bf16((slots, hidden_width)),
+            bf16((slots, width)),
+            bf16((width, hidden_width)),
+        ),
         [
             f32(2 * slots * chunks, LANES),
             half(slots, width),
-            half(width, hidden_width),
-            sems(hidden_width // (2 * LANES)),
+            sems(hidden_width // (4 * LANES)),
         ],
         2 * slots * width * hidden_width,
         2 * width * hidden_width + 6 * slots * width + 2 * slots * hidden_width,
         hbm=(1,),
     )(received, up_weight[0])
-    core = lax.axis_index("core").astype(jnp.int32).reshape(1)
-    share = hidden_width // CORES
-    partial = call(
-        functools.partial(grad_kernel, experts, capacity, factor),
-        bf16((share, width)),
-        [
-            f32(2 * slots * chunks, LANES),
-            half(slots, width),
-            half(CORES * slots, width),
-            half(width, share),
-            half(share, width),
-            sems(share // LANES),
-            sems(share // (2 * LANES)),
-        ],
-        3 * slots * width * hidden_width,
-        width * hidden_width + 6 * slots * width + 2 * share * width,
+    ring = lax.axis_size("y")
+    far, near = ring // 2, (ring - 1) // 2
+    place = jnp.stack([lax.axis_index("y"), lax.axis_index("core"), ring]).astype(jnp.int32)
+    block = (hidden_width // (ring * CORES), width)
+    firsts = (far, ring - near)
+    rest = tuple(i for i in range(ring) if i not in firsts)
+    upward, downward, rows, cots = call(
+        functools.partial(first_grad_kernel, experts, capacity, factor, firsts),
+        (bf16(block), bf16(block), bf16((slots, width)), bf16((CORES * slots, width))),
+        [f32(2 * slots * chunks, LANES)],
+        3 * slots * width * hidden_width * 2 // ring,
+        8 * slots * width,
         smem=(0,),
-        hbm=(4,),
-        out_hbm=True,
-    )(core, hidden, cots, other, up_weight[0])
-    down_grad = lax.psum_scatter(partial, "y", scatter_dimension=0, tiled=True)
-    hidden, partial = lax.optimization_barrier((hidden, partial))
-    out = call(
-        functools.partial(down_kernel, experts, capacity),
-        bf16((slots * chunks, LANES)),
+    )(place, hidden, cots, other, up)
+    parts, out = call(
+        functools.partial(rest_kernel, experts, capacity, factor, rest),
+        (bf16((len(rest),) + block), bf16((slots * chunks, LANES))),
         [
             f32(slots * chunks, LANES),
             half(hidden_width, width),
             sems(width // (2 * LANES)),
         ],
-        2 * slots * width * hidden_width,
-        2 * width * hidden_width + 2 * slots * width + 2 * slots * hidden_width,
-        hbm=(1,),
-    )(hidden, down_weight[0])
+        5 * slots * width * hidden_width,
+        2 * width * hidden_width + 8 * slots * width,
+        smem=(0,),
+        hbm=(5,),
+    )(place, hidden, rows, cots, up, down_weight[0])
+    after = [(i, (i + 1) % ring) for i in range(ring)]
+    before = [(i, (i - 1) % ring) for i in range(ring)]
+
+    def add(*terms):
+        return sum(term.astype(jnp.float32) for term in terms)
+
+    total = parts[rest.index(0)]
+    for hop in range(far):
+        upward = lax.ppermute(upward, "y", after)
+        if hop < near:
+            downward = lax.ppermute(downward, "y", before)
+        if hop < far - 1:
+            upward = add(upward, parts[rest.index(far - 1 - hop)]).astype(jnp.bfloat16)
+        if hop < near - 1:
+            downward = add(downward, parts[rest.index(ring - near + 1 + hop)]).astype(jnp.bfloat16)
+    down_grad = add(total, upward, downward).astype(jnp.bfloat16)
     returned = lax.all_to_all(
         out.reshape(experts, -1, LANES), "expert", split_axis=0, concat_axis=0, tiled=True
     ).reshape(-1, LANES)

time: 134 us -> 129 us (0.963); the launches traced: 134 us -> 127 us
  blocking collectives: 98.4 us -> 65 us
  starting transfers between devices: 1.95 us -> 32.5 us
  between operations: 14.1 us -> 0.8 us
  waiting for transfers between devices: 3.75 us -> 12.5 us
  other arithmetic: 0 us -> 1.34 us
    all_to_all x1 -> x0, blocking collectives: 33.4 us -> none  [on_device(): lax.all_to_all(out.reshape(experts, -1, LANES), 'expert', split_axis=0, c...]
    ppermute x0 -> x7, starting transfers between devices: none -> 23.9 us  [the longest x3 12.9 us: on_device(): downward = lax.ppermute(downward, 'y', before)]
    ppermute x0 -> x7, waiting for transfers between devices: none -> 12.5 us  [the longest x4 9.12 us: on_device(): upward = lax.ppermute(upward, 'y', after)]
    all_to_all x0 -> x1, starting transfers between devices: none -> 6.67 us  [on_device(): lax.all_to_all(out.reshape(experts, -1, LANES), 'expert', split_axis=0, c...]
    reduce_scatter x1 -> x0, waiting for transfers between devices: 3.73 us -> none  [on_device(): down_grad = lax.psum_scatter(partial, 'y', scatter_dimension=0, tiled=True)]
  transfers between devices with their start and end apart: 2 -> 9, of which waited for: 1 -> 5; matrix products, arithmetic and copies ran while one was open for 0% -> 1% of each run, Pallas kernels for 6% -> 8%
where the time goes in v3:
time: 129 us; the launch traced here: 127 us
  blocking collectives  65 us (50%)
  starting transfers between devices  32.5 us (25%)
  Pallas kernels  14.8 us (11%)
  waiting for transfers between devices  12.5 us (10%)
  other arithmetic  1.34 us (1%)
    all_to_all x1, blocking collectives, on_device(): lax.all_to_all(sent.reshape(experts, -1, LANES), 'expert', split_axis=0,...  65 us
    pallas_call x5, Pallas kernels, run(): pl.pallas_call(kernel, out_shape=out_shape, in_specs=[spec(i) for i in ra...  14.8 us
    ppermute x3, starting transfers between devices, on_device(): downward = lax.ppermute(downward, 'y', before)  12.9 us
    ppermute x4, starting transfers between devices, on_device(): upward = lax.ppermute(upward, 'y', after)  11 us
    ppermute x4, waiting for transfers between devices, on_device(): upward = lax.ppermute(upward, 'y', after)  9.12 us
    all_to_all x1, starting transfers between devices, on_device(): lax.all_to_all(out.reshape(experts, -1, LANES), 'expert', split_axis=0, c...  6.67 us
    ppermute x3, waiting for transfers between devices, on_device(): downward = lax.ppermute(downward, 'y', before)  3.34 us
  transfers between devices with their start and end apart: 9, of which 5 were waited for; matrix products, arithmetic and copies ran while one was open for 1% of the time, Pallas kernels for 8%

profile of v3, /device:TPU:6, one launch (start us, length us, event | category | flops | bytes accessed | tf_op | source)
XLA Modules:
  0.0 126.9 jit_solution(6317841295393027431)
XLA Ops:
  0.6 1.8 %shard_map.77 = bf16[3072,128]{1,0:T(8,128)(2,1)S(1)} custom-call(s32[1,128]{1,0:T(1,128)} %bitcast.34, f32[1,128]{1,0:T(1,128)} %bitcast.36, bf16[128,1024]{1,0:T(8,128)(2,1)} %latent_hbm.1, bf16[128,1024]{1,0:T(8,128)(2,1)} %cot_hbm.1), custom_call_target="tpu_custom_call" | custom-call | flops 100663296 | bytes 1310720 | tf_op jit(solution)/shard_map/pallas_call | solution.py:216
  2.5 65.0 %all_to_all.10 = bf16[64,48,128]{2,1,0:T(8,128)(2,1)S(1)} all-to-all(bf16[64,48,128]{2,1,0:T(8,128)(2,1)S(1)} %bitcast.32), channel_id=1, replica_groups=mesh['expert'=64,'y'=8,'core'=2] {'expert'}, dimensions={0} | all-to-all | bytes 1572864 | tf_op jit(solution)/shard_map/all_to_all | solution.py:259
  67.5 1.9 %collective-permute-start = (bf16[3072,128]{1,0:T(8,128)(2,1)S(1)}, bf16[3072,128]{1,0:T(8,128)(2,1)S(1)}, u32[]{:S(2)}, u32[]{:S(2)}) collective-permute-start(bf16[3072,128]{1,0:T(8,128)(2,1)S(1)} %bitcast.30), channel_id=1, source_target_pairs={{0,1},{1,0},{2,3},{3,2},{4,5},{5,4},{6,7},{7,6},{8,9},{9,8},{10,11... | collective-permute-start | bytes 2359304 | tf_op jit(solution)/shard_map/ppermute | solution.py:262
  69.4 0.1 pad_add_fusion.place_ref
  69.5 2.8 %shard_map.78 = (bf16[192,2048]{1,0:T(8,128)(2,1)S(1)}, bf16[192,1024]{1,0:T(8,128)(2,1)S(1)}, bf16[1024,2048]{1,0:T(8,128)(2,1)S(1)}) custom-call(bf16[3072,128]{1,0:T(8,128)(2,1)S(1)} %bitcast.31, bf16[1024,2048]{1,0:T(8,128)(2,1)} %bitcast.38), custom_call_target="tpu_custom_call" | custom-call | flops 805306368 | bytes 6160384 | tf_op jit(solution)/shard_map/pallas_call | solution.py:216
  72.3 0.0 collective-permute-done.other_ref
  72.3 2.0 %shard_map.79 = (bf16[128,1024]{1,0:T(8,128)(2,1)S(1)}, bf16[128,1024]{1,0:T(8,128)(2,1)S(1)}, bf16[192,1024]{1,0:T(8,128)(2,1)S(1)}, bf16[384,1024]{1,0:T(8,128)(2,1)S(1)}) custom-call(s32[3]{0:T(128)S(1)} %pad_add_fusion.place_ref, bf16[192,2048]{1,0:T(8,128)(2,1)S(1)} %get-tuple-element.11.hidden_ref, ...), custom_call_target="tpu_custom_call" | custom-call | flops 301989888 | bytes 1572864 | tf_op jit(solution)/shard_map/pallas_call | solution.py:216
  74.3 3.5 %collective-permute-start.1 = (bf16[128,1024]{1,0:T(8,128)(2,1)S(1)}, bf16[128,1024]{1,0:T(8,128)(2,1)S(1)}, u32[]{:S(2)}, u32[]{:S(2)}) collective-permute-start(bf16[128,1024]{1,0:T(8,128)(2,1)S(1)} %get-tuple-element.18), channel_id=1, source_target_pairs={{0,2},{2,4},{4,6},{6,8},{8,10},{10,12},{12,14},{14,0},{1,3},{3,5},... | collective-permute-start | bytes 786440 | tf_op jit(solution)/shard_map/ppermute | solution.py:314
  77.8 3.8 %collective-permute-start.5 = (bf16[128,1024]{1,0:T(8,128)(2,1)S(1)}, bf16[128,1024]{1,0:T(8,128)(2,1)S(1)}, u32[]{:S(2)}, u32[]{:S(2)}) collective-permute-start(bf16[128,1024]{1,0:T(8,128)(2,1)S(1)} %get-tuple-element.19), channel_id=1, source_target_pairs={{0,14},{2,0},{4,2},{6,4},{8,6},{10,8},{12,10},{14,12},{1,15},{3,1}... | collective-permute-start | bytes 786440 | tf_op jit(solution)/shard_map/ppermute | solution.py:316
  81.7 6.9 %shard_map.80 = (bf16[6,128,1024]{2,1,0:T(8,128)(2,1)S(1)}, bf16[1536,128]{1,0:T(8,128)(2,1)}) custom-call(s32[3]{0:T(128)S(1)} %pad_add_fusion.place_ref, bf16[192,2048]{1,0:T(8,128)(2,1)S(1)} %get-tuple-element.11.hidden_ref, bf16[192,1024]{1,0:T(8,128)(2,1)S(1)} %get-tuple-element.14.rows_ref, bf16[384,1024]{1,0:T(8,128)(2,1)S(1)} %get-tuple-element.15.cots_ref, ...), custom_call_target="tpu_custom_call" | custom-call | flops 2013265920 | bytes 5767168 | tf_op jit(solution)/shard_map/pallas_call | solution.py:216
  88.5 0.0 collective-permute-done.1
  88.5 0.1 fusion.4
  88.6 2.0 %collective-permute-start.2 = (bf16[128,1024]{1,0:T(8,128)(2,1)S(1)}, bf16[128,1024]{1,0:T(8,128)(2,1)S(1)}, u32[]{:S(2)}, u32[]{:S(2)}) collective-permute-start(bf16[128,1024]{1,0:T(8,128)(2,1)S(1)} %fusion.4), channel_id=1, source_target_pairs={{0,2},{2,4},{4,6},{6,8},{8,10},{10,12},{12,14},{14,0},{1,3},{3,5},... | collective-permute-start | bytes 786440 | tf_op jit(solution)/shard_map/ppermute | solution.py:314
  90.7 6.7 %all-to-all-start.1 = ((bf16[64,24,128]{2,1,0:T(8,128)(2,1)}), bf16[64,24,128]{2,1,0:T(8,128)(2,1)S(1)}, u32[]{:S(2)}, u32[]{:S(2)}) async-start(bf16[64,24,128]{2,1,0:T(8,128)(2,1)} %bitcast.8), calls=%async_computation.1 | async-start | bytes 786432 | tf_op jit(solution)/shard_map/all_to_all | solution.py:322
  97.3 0.0 collective-permute-done.5
  97.4 2.8 %collective-permute-done.2 = bf16[128,1024]{1,0:T(8,128)(2,1)S(1)} collective-permute-done((bf16[128,1024]{1,0:T(8,128)(2,1)S(1)}, bf16[128,1024]{1,0:T(8,128)(2,1)S(1)}, u32[]{:S(2)}, u32[]{:S(2)}) %collective-permute-start.2) | collective-permute-done | bytes 262176 | tf_op jit(solution)/shard_map/ppermute | solution.py:314
  100.1 0.2 fusion.3
  100.3 0.0 copy-start
  100.3 0.0 copy-start.1
  100.3 1.9 %collective-permute-start.3 = (bf16[128,1024]{1,0:T(8,128)(2,1)S(1)}, bf16[128,1024]{1,0:T(8,128)(2,1)S(1)}, u32[]{:S(2)}, u32[]{:S(2)}) collective-permute-start(bf16[128,1024]{1,0:T(8,128)(2,1)S(1)} %get-tuple-element.22), channel_id=1, source_target_pairs={{0,2},{2,4},{4,6},{6,8},{8,10},{10,12},{12,14},{14,0},{1,3},{3,5},... | collective-permute-start | bytes 786440 | tf_op jit(solution)/shard_map/ppermute | solution.py:314
  102.3 5.1 %collective-permute-start.6 = (bf16[128,1024]{1,0:T(8,128)(2,1)S(1)}, bf16[128,1024]{1,0:T(8,128)(2,1)S(1)}, u32[]{:S(2)}, u32[]{:S(2)}) collective-permute-start(bf16[128,1024]{1,0:T(8,128)(2,1)S(1)} %get-tuple-element.23), channel_id=1, source_target_pairs={{0,14},{2,0},{4,2},{6,4},{8,6},{10,8},{12,10},{14,12},{1,15},{3,1}... | collective-permute-start | bytes 786440 | tf_op jit(solution)/shard_map/ppermute | solution.py:316
  107.4 3.6 %collective-permute-done.3 = bf16[128,1024]{1,0:T(8,128)(2,1)S(1)} collective-permute-done((bf16[128,1024]{1,0:T(8,128)(2,1)S(1)}, bf16[128,1024]{1,0:T(8,128)(2,1)S(1)}, u32[]{:S(2)}, u32[]{:S(2)}) %collective-permute-start.3) | collective-permute-done | bytes 262176 | tf_op jit(solution)/shard_map/ppermute | solution.py:314
  111.0 1.2 collective-permute-done.6
  112.2 0.2 fusion.2
  112.4 3.5 %collective-permute-start.4 = (bf16[128,1024]{1,0:T(8,128)(2,1)S(1)}, bf16[128,1024]{1,0:T(8,128)(2,1)S(1)}, u32[]{:S(2)}, u32[]{:S(2)}) collective-permute-start(bf16[128,1024]{1,0:T(8,128)(2,1)S(1)} %get-tuple-element.20), channel_id=1, source_target_pairs={{0,2},{2,4},{4,6},{6,8},{8,10},{10,12},{12,14},{14,0},{1,3},{3,5},... | collective-permute-start | bytes 786440 | tf_op jit(solution)/shard_map/ppermute | solution.py:314
  115.9 4.0 %collective-permute-start.7 = (bf16[128,1024]{1,0:T(8,128)(2,1)S(1)}, bf16[128,1024]{1,0:T(8,128)(2,1)S(1)}, u32[]{:S(2)}, u32[]{:S(2)}) collective-permute-start(bf16[128,1024]{1,0:T(8,128)(2,1)S(1)} %get-tuple-element.21), channel_id=1, source_target_pairs={{0,14},{2,0},{4,2},{6,4},{8,6},{10,8},{12,10},{14,12},{1,15},{3,1}... | collective-permute-start | bytes 786440 | tf_op jit(solution)/shard_map/ppermute | solution.py:316
  120.0 2.7 %collective-permute-done.4 = bf16[128,1024]{1,0:T(8,128)(2,1)S(1)} collective-permute-done((bf16[128,1024]{1,0:T(8,128)(2,1)S(1)}, bf16[128,1024]{1,0:T(8,128)(2,1)S(1)}, u32[]{:S(2)}, u32[]{:S(2)}) %collective-permute-start.4) | collective-permute-done | bytes 262176 | tf_op jit(solution)/shard_map/ppermute | solution.py:314
  122.7 2.2 %collective-permute-done.7 = bf16[128,1024]{1,0:T(8,128)(2,1)S(1)} collective-permute-done((bf16[128,1024]{1,0:T(8,128)(2,1)S(1)}, bf16[128,1024]{1,0:T(8,128)(2,1)S(1)}, u32[]{:S(2)}, u32[]{:S(2)}) %collective-permute-start.7) | collective-permute-done | bytes 262176 | tf_op jit(solution)/shard_map/ppermute | solution.py:316
  124.8 0.8 fusion.7
  125.7 0.0 all-to-all-done.1
  125.7 0.0 copy-done
  125.7 1.3 shard_map.81
  (1 shorter events, 0.0 us)
Async XLA Ops:
  67.5 4.8 %collective-permute-start = (bf16[3072,128]{1,0:T(8,128)(2,1)S(1)}, bf16[3072,128]{1,0:T(8,128)(2,1)S(1)}, u32[]{:S(2)}, u32[]{:S(2)}) collective-permute-start(bf16[3072,128]{1,0:T(8,128)(2,1)S(1)} %bitcast.30), channel_id=1, source_target_pairs={{0,1},{1,0},{2,3},{3,2},{4,5},{5,4},{6,7},{7,6},{8,9},{9,8},{10,11... | collective-permute-start | bytes 2359304 | tf_op jit(solution)/shard_map/ppermute | solution.py:262
  74.3 14.2 %collective-permute-start.1 = (bf16[128,1024]{1,0:T(8,128)(2,1)S(1)}, bf16[128,1024]{1,0:T(8,128)(2,1)S(1)}, u32[]{:S(2)}, u32[]{:S(2)}) collective-permute-start(bf16[128,1024]{1,0:T(8,128)(2,1)S(1)} %get-tuple-element.18), channel_id=1, source_target_pairs={{0,2},{2,4},{4,6},{6,8},{8,10},{10,12},{12,14},{14,0},{1,3},{3,5},... | collective-permute-start | bytes 786440 | tf_op jit(solution)/shard_map/ppermute | solution.py:314
  77.8 19.5 %collective-permute-start.5 = (bf16[128,1024]{1,0:T(8,128)(2,1)S(1)}, bf16[128,1024]{1,0:T(8,128)(2,1)S(1)}, u32[]{:S(2)}, u32[]{:S(2)}) collective-permute-start(bf16[128,1024]{1,0:T(8,128)(2,1)S(1)} %get-tuple-element.19), channel_id=1, source_target_pairs={{0,14},{2,0},{4,2},{6,4},{8,6},{10,8},{12,10},{14,12},{1,15},{3,1}... | collective-permute-start | bytes 786440 | tf_op jit(solution)/shard_map/ppermute | solution.py:316
  88.6 11.5 %collective-permute-start.2 = (bf16[128,1024]{1,0:T(8,128)(2,1)S(1)}, bf16[128,1024]{1,0:T(8,128)(2,1)S(1)}, u32[]{:S(2)}, u32[]{:S(2)}) collective-permute-start(bf16[128,1024]{1,0:T(8,128)(2,1)S(1)} %fusion.4), channel_id=1, source_target_pairs={{0,2},{2,4},{4,6},{6,8},{8,10},{10,12},{12,14},{14,0},{1,3},{3,5},... | collective-permute-start | bytes 786440 | tf_op jit(solution)/shard_map/ppermute | solution.py:314
  90.7 35.0 %all-to-all-start.1 = ((bf16[64,24,128]{2,1,0:T(8,128)(2,1)}), bf16[64,24,128]{2,1,0:T(8,128)(2,1)S(1)}, u32[]{:S(2)}, u32[]{:S(2)}) async-start(bf16[64,24,128]{2,1,0:T(8,128)(2,1)} %bitcast.8), calls=%async_computation.1 | async-start | bytes 786432 | tf_op jit(solution)/shard_map/all_to_all | solution.py:322
  100.3 25.3 %copy-start = (s32[128,1]{0,1:T(1,128)S(1)}, s32[128,1]{0,1:T(1,128)}, u32[]{:S(2)}) copy-start(s32[128,1]{0,1:T(1,128)} %param.8) | copy-start | bytes 1540
  100.3 25.3 %copy-start.1 = (f32[128,1]{0,1:T(1,128)S(1)}, f32[128,1]{0,1:T(1,128)}, u32[]{:S(2)}) copy-start(f32[128,1]{0,1:T(1,128)} %param.9) | copy-start | bytes 1540
  100.3 10.7 %collective-permute-start.3 = (bf16[128,1024]{1,0:T(8,128)(2,1)S(1)}, bf16[128,1024]{1,0:T(8,128)(2,1)S(1)}, u32[]{:S(2)}, u32[]{:S(2)}) collective-permute-start(bf16[128,1024]{1,0:T(8,128)(2,1)S(1)} %get-tuple-element.22), channel_id=1, source_target_pairs={{0,2},{2,4},{4,6},{6,8},{8,10},{10,12},{12,14},{14,0},{1,3},{3,5},... | collective-permute-start | bytes 786440 | tf_op jit(solution)/shard_map/ppermute | solution.py:314
  102.3 9.9 %collective-permute-start.6 = (bf16[128,1024]{1,0:T(8,128)(2,1)S(1)}, bf16[128,1024]{1,0:T(8,128)(2,1)S(1)}, u32[]{:S(2)}, u32[]{:S(2)}) collective-permute-start(bf16[128,1024]{1,0:T(8,128)(2,1)S(1)} %get-tuple-element.23), channel_id=1, source_target_pairs={{0,14},{2,0},{4,2},{6,4},{8,6},{10,8},{12,10},{14,12},{1,15},{3,1}... | collective-permute-start | bytes 786440 | tf_op jit(solution)/shard_map/ppermute | solution.py:316
  112.4 10.2 %collective-permute-start.4 = (bf16[128,1024]{1,0:T(8,128)(2,1)S(1)}, bf16[128,1024]{1,0:T(8,128)(2,1)S(1)}, u32[]{:S(2)}, u32[]{:S(2)}) collective-permute-start(bf16[128,1024]{1,0:T(8,128)(2,1)S(1)} %get-tuple-element.20), channel_id=1, source_target_pairs={{0,2},{2,4},{4,6},{6,8},{8,10},{10,12},{12,14},{14,0},{1,3},{3,5},... | collective-permute-start | bytes 786440 | tf_op jit(solution)/shard_map/ppermute | solution.py:314
  115.9 8.9 %collective-permute-start.7 = (bf16[128,1024]{1,0:T(8,128)(2,1)S(1)}, bf16[128,1024]{1,0:T(8,128)(2,1)S(1)}, u32[]{:S(2)}, u32[]{:S(2)}) collective-permute-start(bf16[128,1024]{1,0:T(8,128)(2,1)S(1)} %get-tuple-element.21), channel_id=1, source_target_pairs={{0,14},{2,0},{4,2},{6,4},{8,6},{10,8},{12,10},{14,12},{1,15},{3,1}... | collective-permute-start | bytes 786440 | tf_op jit(solution)/shard_map/ppermute | solution.py:316

commit v4 on v3

--- a/solution.py
+++ b/solution.py
@@ -8,6 +8,7 @@
 from jax.sharding import Mesh, PartitionSpec as P
 
 LANES = 128
+ADD_WEIGHT = 20000
 CORES = 2
 VMEM_LIMIT = 24 * 1024 * 1024
 
@@ -92,17 +93,23 @@
         hidden_ref[:, at] = activation(rows[...], up_ref[:, at])
 
 
-def block_product(factor, place_ref, offset, hidden_ref, rows_ref, cots_ref, up_ref):
-    y = lax.rem(place_ref[0] + offset, place_ref[2])
-    at = pl.ds(pl.multiple_of((CORES * y + place_ref[1]) * LANES, LANES), LANES)
-    other = activation(rows_ref[...], up_ref[:, at])
+def block_products(factor, place_ref, offsets, hidden_ref, rows_ref, cots_ref, up_ref):
+    columns = []
+    for offset in offsets:
+        y = lax.rem(place_ref[0] + offset, place_ref[2])
+        columns.append(pl.ds(pl.multiple_of((CORES * y + place_ref[1]) * LANES, LANES), LANES))
+
+    def gather(ref):
+        return jnp.concatenate([ref[:, at] for at in columns], axis=1)
+
     product = lax.dot_general(
-        jnp.concatenate([hidden_ref[:, at], other], axis=0),
+        jnp.concatenate([gather(hidden_ref), activation(rows_ref[...], gather(up_ref))], axis=0),
         cots_ref[...],
         (((0,), (0,)), ((), ())),
         preferred_element_type=jnp.float32,
     )
-    return (factor * product).astype(jnp.bfloat16)
+    product = (factor * product).astype(jnp.bfloat16)
+    return [product[i * LANES : (i + 1) * LANES] for i in range(len(offsets))]
 
 
 def first_grad_kernel(
@@ -126,10 +133,9 @@
     unpack(stage, rows_ref, 0, sources, capacity, 2, 0)
     unpack(stage, cots_ref, slots, sources, capacity, 2, 1)
     cots_ref[:slots, :] = own_cots_ref[...]
-    for out_ref, offset in zip((up_block_ref, down_block_ref), offsets):
-        out_ref[...] = block_product(
-            factor, place_ref, offset, hidden_ref, rows_ref, cots_ref, up_ref
-        )
+    up_block_ref[...], down_block_ref[...] = block_products(
+        factor, place_ref, offsets, hidden_ref, rows_ref, cots_ref, up_ref
+    )
 
 
 def rest_kernel(
@@ -160,10 +166,12 @@
     ]
     for copy in copies:
         copy.start()
-    for i, offset in enumerate(offsets):
-        part_ref[i] = block_product(
-            factor, place_ref, offset, hidden_ref, rows_ref, cots_ref, up_ref
-        )
+    for i in range(0, len(offsets), 2):
+        pair = offsets[i : i + 2]
+        for j, product in enumerate(
+            block_products(factor, place_ref, pair, hidden_ref, rows_ref, cots_ref, up_ref)
+        ):
+            part_ref[i + j] = product
     for j, copy in enumerate(copies):
         copy.wait()
         out = jnp.dot(
@@ -178,6 +186,12 @@
                     k * sources : (k + 1) * sources, c * LANES : (c + 1) * LANES
                 ]
     out_ref[...] = stage[...].astype(jnp.bfloat16)
+
+
+def add_kernel(index, arrived_ref, part_ref, out_ref):
+    out_ref[...] = (
+        arrived_ref[...].astype(jnp.float32) + part_ref[index].astype(jnp.float32)
+    ).astype(jnp.bfloat16)
 
 
 def mix_kernel(experts, capacity, routes_ref, gates_ref, back_ref, out_ref, stage):
@@ -306,8 +320,14 @@
     after = [(i, (i + 1) % ring) for i in range(ring)]
     before = [(i, (i - 1) % ring) for i in range(ring)]
 
-    def add(*terms):
-        return sum(term.astype(jnp.float32) for term in terms)
+    def add(arrived, offset):
+        return call(
+            functools.partial(add_kernel, rest.index(offset)),
+            bf16(block),
+            [],
+            ADD_WEIGHT * block[0] * block[1],
+            6 * block[0] * block[1],
+        )(arrived, parts)
 
     total = parts[rest.index(0)]
     for hop in range(far):
@@ -315,10 +335,9 @@
         if hop < near:
             downward = lax.ppermute(downward, "y", before)
         if hop < far - 1:
-            upward = add(upward, parts[rest.index(far - 1 - hop)]).astype(jnp.bfloat16)
+            upward = add(upward, far - 1 - hop)
         if hop < near - 1:
-            downward = add(downward, parts[rest.index(ring - near + 1 + hop)]).astype(jnp.bfloat16)
-    down_grad = add(total, upward, downward).astype(jnp.bfloat16)
+            downward = add(downward, ring - near + 1 + hop)
     returned = lax.all_to_all(
         out.reshape(experts, -1, LANES), "expert", split_axis=0, concat_axis=0, tiled=True
     ).reshape(-1, LANES)
@@ -329,6 +348,10 @@
         2 * slots * tokens * width,
         2 * slots * width + 2 * tokens * width,
     )(route_row, gate_row, returned)
+    mixed, upward, downward = lax.optimization_barrier((mixed, upward, downward))
+    down_grad = sum(term.astype(jnp.float32) for term in (total, upward, downward)).astype(
+        jnp.bfloat16
+    )
     return mixed, down_grad[None]
 
 

time: 129 us -> 127 us (0.984); the launches traced: 127 us -> 126 us
    ppermute x3, waiting for transfers between devices: 3.34 us -> 7.21 us  [on_device(): downward = lax.ppermute(downward, 'y', before)]
    ppermute x4, waiting for transfers between devices: 9.12 us -> 5.68 us  [on_device(): upward = lax.ppermute(upward, 'y', after)]
    ppermute x3, starting transfers between devices: 12.9 us -> 14.7 us  [on_device(): downward = lax.ppermute(downward, 'y', before)]
    ppermute x4, starting transfers between devices: 11 us -> 9.37 us  [on_device(): upward = lax.ppermute(upward, 'y', after)]
    pallas_call x5 -> x10, Pallas kernels: 14.8 us -> 14.1 us  [run(): pl.pallas_call(kernel, out_shape=out_shape, in_specs=[spec(i) for i in ra...]
  transfers between devices with their start and end apart: 9 -> 9, of which waited for: 5 -> 4; matrix products, arithmetic and copies ran while one was open for 1% -> 0% of each run, Pallas kernels for 8% -> 8%
where the time goes in v4:
time: 127 us; the launch traced here: 126 us
  blocking collectives  65 us (51%)
  starting transfers between devices  32.7 us (26%)
  Pallas kernels  14.1 us (11%)
  waiting for transfers between devices  12.9 us (10%)
    all_to_all x1, blocking collectives, on_device(): lax.all_to_all(sent.reshape(experts, -1, LANES), 'expert', split_axis=0,...  65 us
    ppermute x3, starting transfers between devices, on_device(): downward = lax.ppermute(downward, 'y', before)  14.7 us
    pallas_call x10, Pallas kernels, run(): pl.pallas_call(kernel, out_shape=out_shape, in_specs=[spec(i) for i in ra...  14.1 us
    ppermute x4, starting transfers between devices, on_device(): upward = lax.ppermute(upward, 'y', after)  9.37 us
    ppermute x3, waiting for transfers between devices, on_device(): downward = lax.ppermute(downward, 'y', before)  7.21 us
    all_to_all x1, starting transfers between devices, on_device(): lax.all_to_all(out.reshape(experts, -1, LANES), 'expert', split_axis=0, c...  6.68 us
    ppermute x4, waiting for transfers between devices, on_device(): upward = lax.ppermute(upward, 'y', after)  5.68 us
  transfers between devices with their start and end apart: 9, of which 4 were waited for; matrix products, arithmetic and copies ran while one was open for 0% of the time, Pallas kernels for 8%

profile of v4, /device:TPU:6, one launch (start us, length us, event | category | flops | bytes accessed | tf_op | source)
XLA Modules:
  0.0 126.4 jit_solution(12046236241961566004)
XLA Ops:
  0.6 1.8 %shard_map.77 = bf16[3072,128]{1,0:T(8,128)(2,1)S(1)} custom-call(s32[1,128]{1,0:T(1,128)} %bitcast.19, f32[1,128]{1,0:T(1,128)} %bitcast.21, bf16[128,1024]{1,0:T(8,128)(2,1)} %latent_hbm.1, bf16[128,1024]{1,0:T(8,128)(2,1)} %cot_hbm.1), custom_call_target="tpu_custom_call" | custom-call | flops 100663296 | bytes 1310720 | tf_op jit(solution)/shard_map/pallas_call | solution.py:230
  2.5 65.0 %all_to_all.10 = bf16[64,48,128]{2,1,0:T(8,128)(2,1)S(1)} all-to-all(bf16[64,48,128]{2,1,0:T(8,128)(2,1)S(1)} %bitcast.17), channel_id=1, replica_groups=mesh['expert'=64,'y'=8,'core'=2] {'expert'}, dimensions={0} | all-to-all | bytes 1572864 | tf_op jit(solution)/shard_map/all_to_all | solution.py:273
  67.5 1.9 %collective-permute-start = (bf16[3072,128]{1,0:T(8,128)(2,1)S(1)}, bf16[3072,128]{1,0:T(8,128)(2,1)S(1)}, u32[]{:S(2)}, u32[]{:S(2)}) collective-permute-start(bf16[3072,128]{1,0:T(8,128)(2,1)S(1)} %bitcast.15), channel_id=1, source_target_pairs={{0,1},{1,0},{2,3},{3,2},{4,5},{5,4},{6,7},{7,6},{8,9},{9,8},{10,11... | collective-permute-start | bytes 2359304 | tf_op jit(solution)/shard_map/ppermute | solution.py:276
  69.4 0.1 pad_add_fusion.place_ref
  69.5 2.8 %shard_map.78 = (bf16[192,2048]{1,0:T(8,128)(2,1)S(1)}, bf16[192,1024]{1,0:T(8,128)(2,1)S(1)}, bf16[1024,2048]{1,0:T(8,128)(2,1)S(1)}) custom-call(bf16[3072,128]{1,0:T(8,128)(2,1)S(1)} %bitcast.16, bf16[1024,2048]{1,0:T(8,128)(2,1)} %bitcast.23), custom_call_target="tpu_custom_call" | custom-call | flops 805306368 | bytes 6160384 | tf_op jit(solution)/shard_map/pallas_call | solution.py:230
  72.3 0.0 collective-permute-done.other_ref
  72.3 1.7 %shard_map.79 = (bf16[128,1024]{1,0:T(8,128)(2,1)S(1)}, bf16[128,1024]{1,0:T(8,128)(2,1)S(1)}, bf16[192,1024]{1,0:T(8,128)(2,1)S(1)}, bf16[384,1024]{1,0:T(8,128)(2,1)S(1)}) custom-call(s32[3]{0:T(128)S(1)} %pad_add_fusion.place_ref, bf16[192,2048]{1,0:T(8,128)(2,1)S(1)} %get-tuple-element.14.hidden_ref, ...), custom_call_target="tpu_custom_call" | custom-call | flops 301989888 | bytes 1572864 | tf_op jit(solution)/shard_map/pallas_call | solution.py:230
  74.1 3.5 %collective-permute-start.1 = (bf16[128,1024]{1,0:T(8,128)(2,1)S(1)}, bf16[128,1024]{1,0:T(8,128)(2,1)S(1)}, u32[]{:S(2)}, u32[]{:S(2)}) collective-permute-start(bf16[128,1024]{1,0:T(8,128)(2,1)S(1)} %get-tuple-element.20), channel_id=1, source_target_pairs={{0,2},{2,4},{4,6},{6,8},{8,10},{10,12},{12,14},{14,0},{1,3},{3,5},... | collective-permute-start | bytes 786440 | tf_op jit(solution)/shard_map/ppermute | solution.py:334
  77.5 6.2 %shard_map.80 = (bf16[6,128,1024]{2,1,0:T(8,128)(2,1)S(1)}, bf16[1536,128]{1,0:T(8,128)(2,1)}) custom-call(s32[3]{0:T(128)S(1)} %pad_add_fusion.place_ref, bf16[192,2048]{1,0:T(8,128)(2,1)S(1)} %get-tuple-element.14.hidden_ref, bf16[192,1024]{1,0:T(8,128)(2,1)S(1)} %get-tuple-element.17.rows_ref, bf16[384,1024]{1,0:T(8,128)(2,1)S(1)} %get-tuple-element.18.cots_ref, ...), custom_call_target="tpu_custom_call" | custom-call | flops 2013265920 | bytes 5767168 | tf_op jit(solution)/shard_map/pallas_call | solution.py:230
  83.7 6.7 %all-to-all-start.1 = ((bf16[64,24,128]{2,1,0:T(8,128)(2,1)}), bf16[64,24,128]{2,1,0:T(8,128)(2,1)S(1)}, u32[]{:S(2)}, u32[]{:S(2)}) async-start(bf16[64,24,128]{2,1,0:T(8,128)(2,1)} %bitcast.8), calls=%async_computation.1 | async-start | bytes 786432 | tf_op jit(solution)/shard_map/all_to_all | solution.py:341
  90.4 3.8 %collective-permute-start.5 = (bf16[128,1024]{1,0:T(8,128)(2,1)S(1)}, bf16[128,1024]{1,0:T(8,128)(2,1)S(1)}, u32[]{:S(2)}, u32[]{:S(2)}) collective-permute-start(bf16[128,1024]{1,0:T(8,128)(2,1)S(1)} %get-tuple-element.22), channel_id=1, source_target_pairs={{0,14},{2,0},{4,2},{6,4},{8,6},{10,8},{12,10},{14,12},{1,15},{3,1}... | collective-permute-start | bytes 786440 | tf_op jit(solution)/shard_map/ppermute | solution.py:336
  94.2 0.0 collective-permute-done.1.arrived_ref
  94.2 0.1 shard_map.82
  94.3 2.0 %collective-permute-start.2 = (bf16[128,1024]{1,0:T(8,128)(2,1)S(1)}, bf16[128,1024]{1,0:T(8,128)(2,1)S(1)}, u32[]{:S(2)}, u32[]{:S(2)}) collective-permute-start(bf16[128,1024]{1,0:T(8,128)(2,1)S(1)} %shard_map.82), channel_id=1, source_target_pairs={{0,2},{2,4},{4,6},{6,8},{8,10},{10,12},{12,14},{14,0},{1,3},{3,5},... | collective-permute-start | bytes 786440 | tf_op jit(solution)/shard_map/ppermute | solution.py:334
  96.3 3.8 %collective-permute-done.5.arrived_ref = bf16[128,1024]{1,0:T(8,128)(2,1)S(1)} collective-permute-done((bf16[128,1024]{1,0:T(8,128)(2,1)S(1)}, bf16[128,1024]{1,0:T(8,128)(2,1)S(1)}, u32[]{:S(2)}, u32[]{:S(2)}) %collective-permute-start.5) | collective-permute-done | bytes 262176 | tf_op jit(solution)/shard_map/ppermute | solution.py:336
  100.2 0.1 shard_map.85
  100.2 5.3 %collective-permute-start.6 = (bf16[128,1024]{1,0:T(8,128)(2,1)S(1)}, bf16[128,1024]{1,0:T(8,128)(2,1)S(1)}, u32[]{:S(2)}, u32[]{:S(2)}) collective-permute-start(bf16[128,1024]{1,0:T(8,128)(2,1)S(1)} %shard_map.85), channel_id=1, source_target_pairs={{0,14},{2,0},{4,2},{6,4},{8,6},{10,8},{12,10},{14,12},{1,15},{3,1}... | collective-permute-start | bytes 786440 | tf_op jit(solution)/shard_map/ppermute | solution.py:336
  105.5 0.0 collective-permute-done.2.arrived_ref
  105.5 0.1 shard_map.83
  105.6 1.9 %collective-permute-start.3 = (bf16[128,1024]{1,0:T(8,128)(2,1)S(1)}, bf16[128,1024]{1,0:T(8,128)(2,1)S(1)}, u32[]{:S(2)}, u32[]{:S(2)}) collective-permute-start(bf16[128,1024]{1,0:T(8,128)(2,1)S(1)} %shard_map.83), channel_id=1, source_target_pairs={{0,2},{2,4},{4,6},{6,8},{8,10},{10,12},{12,14},{14,0},{1,3},{3,5},... | collective-permute-start | bytes 786440 | tf_op jit(solution)/shard_map/ppermute | solution.py:334
  107.5 2.8 %collective-permute-done.6.arrived_ref = bf16[128,1024]{1,0:T(8,128)(2,1)S(1)} collective-permute-done((bf16[128,1024]{1,0:T(8,128)(2,1)S(1)}, bf16[128,1024]{1,0:T(8,128)(2,1)S(1)}, u32[]{:S(2)}, u32[]{:S(2)}) %collective-permute-start.6) | collective-permute-done | bytes 262176 | tf_op jit(solution)/shard_map/ppermute | solution.py:336
  110.3 0.1 shard_map.86
  110.4 0.0 copy-start
  110.4 0.0 copy-start.1
  110.4 5.6 %collective-permute-start.7 = (bf16[128,1024]{1,0:T(8,128)(2,1)S(1)}, bf16[128,1024]{1,0:T(8,128)(2,1)S(1)}, u32[]{:S(2)}, u32[]{:S(2)}) collective-permute-start(bf16[128,1024]{1,0:T(8,128)(2,1)S(1)} %shard_map.86), channel_id=1, source_target_pairs={{0,14},{2,0},{4,2},{6,4},{8,6},{10,8},{12,10},{14,12},{1,15},{3,1}... | collective-permute-start | bytes 786440 | tf_op jit(solution)/shard_map/ppermute | solution.py:336
  116.0 0.0 collective-permute-done.3.arrived_ref
  116.1 0.1 shard_map.84
  116.1 1.9 %collective-permute-start.4 = (bf16[128,1024]{1,0:T(8,128)(2,1)S(1)}, bf16[128,1024]{1,0:T(8,128)(2,1)S(1)}, u32[]{:S(2)}, u32[]{:S(2)}) collective-permute-start(bf16[128,1024]{1,0:T(8,128)(2,1)S(1)} %shard_map.84), channel_id=1, source_target_pairs={{0,2},{2,4},{4,6},{6,8},{8,10},{10,12},{12,14},{14,0},{1,3},{3,5},... | collective-permute-start | bytes 786440 | tf_op jit(solution)/shard_map/ppermute | solution.py:334
  118.1 1.3 shard_map.81
  119.3 0.6 collective-permute-done.7
  119.9 5.7 %collective-permute-done.4 = bf16[128,1024]{1,0:T(8,128)(2,1)S(1)} collective-permute-done((bf16[128,1024]{1,0:T(8,128)(2,1)S(1)}, bf16[128,1024]{1,0:T(8,128)(2,1)S(1)}, u32[]{:S(2)}, u32[]{:S(2)}) %collective-permute-start.4) | collective-permute-done | bytes 262176 | tf_op jit(solution)/shard_map/ppermute | solution.py:334
  125.6 0.8 fusion.2
  (3 shorter events, 0.0 us)
Async XLA Ops:
  67.5 4.8 %collective-permute-start = (bf16[3072,128]{1,0:T(8,128)(2,1)S(1)}, bf16[3072,128]{1,0:T(8,128)(2,1)S(1)}, u32[]{:S(2)}, u32[]{:S(2)}) collective-permute-start(bf16[3072,128]{1,0:T(8,128)(2,1)S(1)} %bitcast.15), channel_id=1, source_target_pairs={{0,1},{1,0},{2,3},{3,2},{4,5},{5,4},{6,7},{7,6},{8,9},{9,8},{10,11... | collective-permute-start | bytes 2359304 | tf_op jit(solution)/shard_map/ppermute | solution.py:276
  74.1 20.2 %collective-permute-start.1 = (bf16[128,1024]{1,0:T(8,128)(2,1)S(1)}, bf16[128,1024]{1,0:T(8,128)(2,1)S(1)}, u32[]{:S(2)}, u32[]{:S(2)}) collective-permute-start(bf16[128,1024]{1,0:T(8,128)(2,1)S(1)} %get-tuple-element.20), channel_id=1, source_target_pairs={{0,2},{2,4},{4,6},{6,8},{8,10},{10,12},{12,14},{14,0},{1,3},{3,5},... | collective-permute-start | bytes 786440 | tf_op jit(solution)/shard_map/ppermute | solution.py:334
  83.7 34.3 %all-to-all-start.1 = ((bf16[64,24,128]{2,1,0:T(8,128)(2,1)}), bf16[64,24,128]{2,1,0:T(8,128)(2,1)S(1)}, u32[]{:S(2)}, u32[]{:S(2)}) async-start(bf16[64,24,128]{2,1,0:T(8,128)(2,1)} %bitcast.8), calls=%async_computation.1 | async-start | bytes 786432 | tf_op jit(solution)/shard_map/all_to_all | solution.py:341
  90.4 9.8 %collective-permute-start.5 = (bf16[128,1024]{1,0:T(8,128)(2,1)S(1)}, bf16[128,1024]{1,0:T(8,128)(2,1)S(1)}, u32[]{:S(2)}, u32[]{:S(2)}) collective-permute-start(bf16[128,1024]{1,0:T(8,128)(2,1)S(1)} %get-tuple-element.22), channel_id=1, source_target_pairs={{0,14},{2,0},{4,2},{6,4},{8,6},{10,8},{12,10},{14,12},{1,15},{3,1}... | collective-permute-start | bytes 786440 | tf_op jit(solution)/shard_map/ppermute | solution.py:336
  94.3 11.3 %collective-permute-start.2 = (bf16[128,1024]{1,0:T(8,128)(2,1)S(1)}, bf16[128,1024]{1,0:T(8,128)(2,1)S(1)}, u32[]{:S(2)}, u32[]{:S(2)}) collective-permute-start(bf16[128,1024]{1,0:T(8,128)(2,1)S(1)} %shard_map.82), channel_id=1, source_target_pairs={{0,2},{2,4},{4,6},{6,8},{8,10},{10,12},{12,14},{14,0},{1,3},{3,5},... | collective-permute-start | bytes 786440 | tf_op jit(solution)/shard_map/ppermute | solution.py:334
  100.2 10.1 %collective-permute-start.6 = (bf16[128,1024]{1,0:T(8,128)(2,1)S(1)}, bf16[128,1024]{1,0:T(8,128)(2,1)S(1)}, u32[]{:S(2)}, u32[]{:S(2)}) collective-permute-start(bf16[128,1024]{1,0:T(8,128)(2,1)S(1)} %shard_map.85), channel_id=1, source_target_pairs={{0,14},{2,0},{4,2},{6,4},{8,6},{10,8},{12,10},{14,12},{1,15},{3,1}... | collective-permute-start | bytes 786440 | tf_op jit(solution)/shard_map/ppermute | solution.py:336
  105.6 10.4 %collective-permute-start.3 = (bf16[128,1024]{1,0:T(8,128)(2,1)S(1)}, bf16[128,1024]{1,0:T(8,128)(2,1)S(1)}, u32[]{:S(2)}, u32[]{:S(2)}) collective-permute-start(bf16[128,1024]{1,0:T(8,128)(2,1)S(1)} %shard_map.83), channel_id=1, source_target_pairs={{0,2},{2,4},{4,6},{6,8},{8,10},{10,12},{12,14},{14,0},{1,3},{3,5},... | collective-permute-start | bytes 786440 | tf_op jit(solution)/shard_map/ppermute | solution.py:334
  110.4 7.7 %copy-start = (s32[128,1]{0,1:T(1,128)S(1)}, s32[128,1]{0,1:T(1,128)}, u32[]{:S(2)}) copy-start(s32[128,1]{0,1:T(1,128)} %param.8) | copy-start | bytes 1540
  110.4 7.7 %copy-start.1 = (f32[128,1]{0,1:T(1,128)S(1)}, f32[128,1]{0,1:T(1,128)}, u32[]{:S(2)}) copy-start(f32[128,1]{0,1:T(1,128)} %param.9) | copy-start | bytes 1540
  110.4 9.5 %collective-permute-start.7 = (bf16[128,1024]{1,0:T(8,128)(2,1)S(1)}, bf16[128,1024]{1,0:T(8,128)(2,1)S(1)}, u32[]{:S(2)}, u32[]{:S(2)}) collective-permute-start(bf16[128,1024]{1,0:T(8,128)(2,1)S(1)} %shard_map.86), channel_id=1, source_target_pairs={{0,14},{2,0},{4,2},{6,4},{8,6},{10,8},{12,10},{14,12},{1,15},{3,1}... | collective-permute-start | bytes 786440 | tf_op jit(solution)/shard_map/ppermute | solution.py:336
  116.1 9.5 %collective-permute-start.4 = (bf16[128,1024]{1,0:T(8,128)(2,1)S(1)}, bf16[128,1024]{1,0:T(8,128)(2,1)S(1)}, u32[]{:S(2)}, u32[]{:S(2)}) collective-permute-start(bf16[128,1024]{1,0:T(8,128)(2,1)S(1)} %shard_map.84), channel_id=1, source_target_pairs={{0,2},{2,4},{4,6},{6,8},{8,10},{10,12},{12,14},{14,0},{1,3},{3,5},... | collective-permute-start | bytes 786440 | tf_op jit(solution)/shard_map/ppermute | solution.py:334

commit v5 on v4

--- a/solution.py
+++ b/solution.py
@@ -93,26 +93,7 @@
         hidden_ref[:, at] = activation(rows[...], up_ref[:, at])
 
 
-def block_products(factor, place_ref, offsets, hidden_ref, rows_ref, cots_ref, up_ref):
-    columns = []
-    for offset in offsets:
-        y = lax.rem(place_ref[0] + offset, place_ref[2])
-        columns.append(pl.ds(pl.multiple_of((CORES * y + place_ref[1]) * LANES, LANES), LANES))
-
-    def gather(ref):
-        return jnp.concatenate([ref[:, at] for at in columns], axis=1)
-
-    product = lax.dot_general(
-        jnp.concatenate([gather(hidden_ref), activation(rows_ref[...], gather(up_ref))], axis=0),
-        cots_ref[...],
-        (((0,), (0,)), ((), ())),
-        preferred_element_type=jnp.float32,
-    )
-    product = (factor * product).astype(jnp.bfloat16)
-    return [product[i * LANES : (i + 1) * LANES] for i in range(len(offsets))]
-
-
-def first_grad_kernel(
+def grad_kernel(
     sources,
     capacity,
     factor,
@@ -122,69 +103,53 @@
     own_cots_ref,
     other_ref,
     up_ref,
+    down_hbm,
     up_block_ref,
     down_block_ref,
-    rows_ref,
-    cots_ref,
+    part_ref,
+    down_ref,
     stage,
+    rows,
+    cots,
+    acts,
+    sem,
 ):
+    fetch = pltpu.make_async_copy(down_hbm, down_ref, sem)
+    fetch.start()
     slots = sources * capacity
     stage[...] = other_ref[...].astype(jnp.float32)
-    unpack(stage, rows_ref, 0, sources, capacity, 2, 0)
-    unpack(stage, cots_ref, slots, sources, capacity, 2, 1)
-    cots_ref[:slots, :] = own_cots_ref[...]
-    up_block_ref[...], down_block_ref[...] = block_products(
-        factor, place_ref, offsets, hidden_ref, rows_ref, cots_ref, up_ref
-    )
-
-
-def rest_kernel(
-    sources,
-    capacity,
-    factor,
-    offsets,
-    place_ref,
-    hidden_ref,
-    rows_ref,
-    cots_ref,
-    up_ref,
-    down_hbm,
-    part_ref,
-    out_ref,
-    stage,
-    down,
-    sems,
-):
-    width = down.shape[1]
+    unpack(stage, rows, 0, sources, capacity, 2, 0)
+    unpack(stage, cots, slots, sources, capacity, 2, 1)
+    cots[:slots, :] = own_cots_ref[...]
+    for j in range(0, len(offsets), 4):
+        columns = []
+        for offset in offsets[j : j + 4]:
+            y = lax.rem(place_ref[0] + offset, place_ref[2])
+            columns.append(pl.ds(pl.multiple_of((CORES * y + place_ref[1]) * LANES, LANES), LANES))
+        at = pl.ds(j * LANES, 4 * LANES)
+        weight = jnp.concatenate([up_ref[:, column] for column in columns], axis=1)
+        acts[:slots, at] = jnp.concatenate([hidden_ref[:, column] for column in columns], axis=1)
+        acts[slots:, at] = activation(rows[...], weight)
+    product = lax.dot_general(
+        acts[...], cots[...], (((0,), (0,)), ((), ())), preferred_element_type=jnp.float32
+    )
+    product = (factor * product).astype(jnp.bfloat16)
+    up_block_ref[...] = product[:LANES]
+    down_block_ref[...] = product[LANES : 2 * LANES]
+    for j in range(len(offsets) - 2):
+        part_ref[j] = product[(j + 2) * LANES : (j + 3) * LANES]
+    fetch.wait()
+
+
+def down_kernel(sources, capacity, hidden_ref, down_ref, out_ref, stage):
+    width = down_ref.shape[1]
     chunks = width // LANES
-    tile = 2 * LANES
-    copies = [
-        pltpu.make_async_copy(
-            down_hbm.at[:, pl.ds(j * tile, tile)], down.at[:, pl.ds(j * tile, tile)], sems.at[j]
-        )
-        for j in range(width // tile)
-    ]
-    for copy in copies:
-        copy.start()
-    for i in range(0, len(offsets), 2):
-        pair = offsets[i : i + 2]
-        for j, product in enumerate(
-            block_products(factor, place_ref, pair, hidden_ref, rows_ref, cots_ref, up_ref)
-        ):
-            part_ref[i + j] = product
-    for j, copy in enumerate(copies):
-        copy.wait()
-        out = jnp.dot(
-            hidden_ref[...],
-            down[:, j * tile : (j + 1) * tile],
-            preferred_element_type=jnp.float32,
-        )
-        for k in range(capacity):
-            for c in range(tile // LANES):
-                first = k * chunks + j * (tile // LANES) + c
-                stage[pl.ds(first, sources, stride=capacity * chunks), :] = out[
-                    k * sources : (k + 1) * sources, c * LANES : (c + 1) * LANES
-                ]
+    out = jnp.dot(hidden_ref[...], down_ref[...], preferred_element_type=jnp.float32)
+    for k in range(capacity):
+        for c in range(chunks):
+            stage[pl.ds(k * chunks + c, sources, stride=capacity * chunks), :] = out[
+                k * sources : (k + 1) * sources, c * LANES : (c + 1) * LANES
+            ]
     out_ref[...] = stage[...].astype(jnp.bfloat16)
 
 
@@ -296,27 +261,33 @@
     block = (hidden_width // (ring * CORES), width)
     firsts = (far, ring - near)
     rest = tuple(i for i in range(ring) if i not in firsts)
-    upward, downward, rows, cots = call(
-        functools.partial(first_grad_kernel, experts, capacity, factor, firsts),
-        (bf16(block), bf16(block), bf16((slots, width)), bf16((CORES * slots, width))),
-        [f32(2 * slots * chunks, LANES)],
-        3 * slots * width * hidden_width * 2 // ring,
-        8 * slots * width,
-        smem=(0,),
-    )(place, hidden, cots, other, up)
-    parts, out = call(
-        functools.partial(rest_kernel, experts, capacity, factor, rest),
-        (bf16((len(rest),) + block), bf16((slots * chunks, LANES))),
+    upward, downward, parts, down = call(
+        functools.partial(grad_kernel, experts, capacity, factor, firsts + rest),
+        (
+            bf16(block),
+            bf16(block),
+            bf16((len(rest),) + block),
+            bf16((hidden_width, width)),
+        ),
         [
-            f32(slots * chunks, LANES),
-            half(hidden_width, width),
-            sems(width // (2 * LANES)),
+            f32(2 * slots * chunks, LANES),
+            half(slots, width),
+            half(CORES * slots, width),
+            half(CORES * slots, hidden_width // CORES),
+            pltpu.SemaphoreType.DMA,
         ],
-        5 * slots * width * hidden_width,
+        3 * slots * width * hidden_width,
         2 * width * hidden_width + 8 * slots * width,
         smem=(0,),
         hbm=(5,),
-    )(place, hidden, rows, cots, up, down_weight[0])
+    )(place, hidden, cots, other, up, down_weight[0])
+    out = call(
+        functools.partial(down_kernel, experts, capacity),
+        bf16((slots * chunks, LANES)),
+        [f32(slots * chunks, LANES)],
+        2 * slots * width * hidden_width,
+        2 * width * hidden_width + 4 * slots * width,
+    )(hidden, down)
     after = [(i, (i + 1) % ring) for i in range(ring)]
     before = [(i, (i - 1) % ring) for i in range(ring)]
 
@@ -332,10 +303,12 @@
     total = parts[rest.index(0)]
     for hop in range(far):
         upward = lax.ppermute(upward, "y", after)
-        if hop < near:
-            downward = lax.ppermute(downward, "y", before)
+        if hop == 0:
+            upward, downward = lax.optimization_barrier((upward, downward))
         if hop < far - 1:
             upward = add(upward, far - 1 - hop)
+    for hop in range(near):
+        downward = lax.ppermute(downward, "y", before)
         if hop < near - 1:
             downward = add(downward, ring - near + 1 + hop)
     returned = lax.all_to_all(

time: 127 us -> 125 us (0.984)
  the two profiles are of different devices: /device:TPU:6 before, /device:TPU:30 now
where the time goes in v5:
time: 125 us
  blocking collectives  65 us (52%)
  starting transfers between devices  33.2 us (27%)
  waiting for transfers between devices  12.8 us (10%)
  Pallas kernels  11.8 us (9%)
    all_to_all x1, blocking collectives, on_device(): lax.all_to_all(sent.reshape(experts, -1, LANES), 'expert', split_axis=0,...  65 us
    ppermute x4, starting transfers between devices, on_device(): upward = lax.ppermute(upward, 'y', after)  18.3 us
    pallas_call x10, Pallas kernels, run(): pl.pallas_call(kernel, out_shape=out_shape, in_specs=[spec(i) for i in ra...  11.8 us
    ppermute x4, waiting for transfers between devices, on_device(): upward = lax.ppermute(upward, 'y', after)  7.14 us
    all_to_all x1, starting transfers between devices, on_device(): lax.all_to_all(out.reshape(experts, -1, LANES), 'expert', split_axis=0, c...  6.65 us
    ppermute x3, starting transfers between devices, on_device(): downward = lax.ppermute(downward, 'y', before)  6.32 us
    ppermute x3, waiting for transfers between devices, on_device(): downward = lax.ppermute(downward, 'y', before)  5.69 us
  transfers between devices with their start and end apart: 9, of which 4 were waited for; matrix products, arithmetic and copies ran while one was open for 0% of the time, Pallas kernels for 5%

profile of v5, /device:TPU:30, one launch (start us, length us, event | category | flops | bytes accessed | tf_op | source)
XLA Modules:
  0.0 124.6 jit_solution(13653663903022294431)
XLA Ops:
  0.6 1.8 %shard_map.77 = bf16[3072,128]{1,0:T(8,128)(2,1)S(1)} custom-call(s32[1,128]{1,0:T(1,128)} %bitcast.19, f32[1,128]{1,0:T(1,128)} %bitcast.21, bf16[128,1024]{1,0:T(8,128)(2,1)} %latent_hbm.1, bf16[128,1024]{1,0:T(8,128)(2,1)} %cot_hbm.1), custom_call_target="tpu_custom_call" | custom-call | flops 100663296 | bytes 1310720 | tf_op jit(solution)/shard_map/pallas_call | solution.py:195
  2.5 65.0 %all_to_all.10 = bf16[64,48,128]{2,1,0:T(8,128)(2,1)S(1)} all-to-all(bf16[64,48,128]{2,1,0:T(8,128)(2,1)S(1)} %bitcast.17), channel_id=1, replica_groups=mesh['expert'=64,'y'=8,'core'=2] {'expert'}, dimensions={0} | all-to-all | bytes 1572864 | tf_op jit(solution)/shard_map/all_to_all | solution.py:238
  67.5 1.9 %collective-permute-start = (bf16[3072,128]{1,0:T(8,128)(2,1)S(1)}, bf16[3072,128]{1,0:T(8,128)(2,1)S(1)}, u32[]{:S(2)}, u32[]{:S(2)}) collective-permute-start(bf16[3072,128]{1,0:T(8,128)(2,1)S(1)} %bitcast.15), channel_id=1, source_target_pairs={{0,1},{1,0},{2,3},{3,2},{4,5},{5,4},{6,7},{7,6},{8,9},{9,8},{10,11... | collective-permute-start | bytes 2359304 | tf_op jit(solution)/shard_map/ppermute | solution.py:241
  69.4 0.1 pad_add_fusion.place_ref
  69.5 2.8 %shard_map.78 = (bf16[192,2048]{1,0:T(8,128)(2,1)S(1)}, bf16[192,1024]{1,0:T(8,128)(2,1)S(1)}, bf16[1024,2048]{1,0:T(8,128)(2,1)S(1)}) custom-call(bf16[3072,128]{1,0:T(8,128)(2,1)S(1)} %bitcast.16, bf16[1024,2048]{1,0:T(8,128)(2,1)} %bitcast.23), custom_call_target="tpu_custom_call" | custom-call | flops 805306368 | bytes 6160384 | tf_op jit(solution)/shard_map/pallas_call | solution.py:195
  72.3 0.0 collective-permute-done.other_ref
  72.3 3.7 %shard_map.79 = (bf16[128,1024]{1,0:T(8,128)(2,1)S(1)}, bf16[128,1024]{1,0:T(8,128)(2,1)S(1)}, bf16[6,128,1024]{2,1,0:T(8,128)(2,1)S(1)}, bf16[2048,1024]{1,0:T(8,128)(2,1)S(1)}) custom-call(s32[3]{0:T(128)S(1)} %pad_add_fusion.place_ref, bf16[192,2048]{1,0:T(8,128)(2,1)S(1)} %get-tuple-element.14.hidden_ref, ...), custom_call_target="tpu_custom_call" | custom-call | flops 1207959552 | bytes 5767168 | tf_op jit(solution)/shard_map/pallas_call | solution.py:195
  76.1 4.7 %collective-permute-start.1 = (bf16[128,1024]{1,0:T(8,128)(2,1)S(1)}, bf16[128,1024]{1,0:T(8,128)(2,1)S(1)}, u32[]{:S(2)}, u32[]{:S(2)}) collective-permute-start(bf16[128,1024]{1,0:T(8,128)(2,1)S(1)} %get-tuple-element.18), channel_id=1, source_target_pairs={{0,2},{2,4},{4,6},{6,8},{8,10},{10,12},{12,14},{14,0},{1,3},{3,5},... | collective-permute-start | bytes 786440 | tf_op jit(solution)/shard_map/ppermute | solution.py:305
  80.8 1.8 %shard_map.80 = bf16[1536,128]{1,0:T(8,128)(2,1)} custom-call(bf16[192,2048]{1,0:T(8,128)(2,1)S(1)} %get-tuple-element.14.hidden_ref, bf16[2048,1024]{1,0:T(8,128)(2,1)S(1)} %get-tuple-element.17.down_ref), custom_call_target="tpu_custom_call" | custom-call | flops 805306368 | bytes 4980736 | tf_op jit(solution)/shard_map/pallas_call | solution.py:195
  82.6 6.6 %all-to-all-start.1 = ((bf16[64,24,128]{2,1,0:T(8,128)(2,1)}), bf16[64,24,128]{2,1,0:T(8,128)(2,1)S(1)}, u32[]{:S(2)}, u32[]{:S(2)}) async-start(bf16[64,24,128]{2,1,0:T(8,128)(2,1)} %bitcast.8), calls=%async_computation.1 | async-start | bytes 786432 | tf_op jit(solution)/shard_map/all_to_all | solution.py:314
  89.3 0.1 shard_map.82
  89.4 3.4 %collective-permute-start.2 = (bf16[128,1024]{1,0:T(8,128)(2,1)S(1)}, bf16[128,1024]{1,0:T(8,128)(2,1)S(1)}, u32[]{:S(2)}, u32[]{:S(2)}) collective-permute-start(bf16[128,1024]{1,0:T(8,128)(2,1)S(1)} %shard_map.82), channel_id=1, source_target_pairs={{0,2},{2,4},{4,6},{6,8},{8,10},{10,12},{12,14},{14,0},{1,3},{3,5},... | collective-permute-start | bytes 786440 | tf_op jit(solution)/shard_map/ppermute | solution.py:305
  92.7 2.5 %collective-permute-start.5 = (bf16[128,1024]{1,0:T(8,128)(2,1)S(1)}, bf16[128,1024]{1,0:T(8,128)(2,1)S(1)}, u32[]{:S(2)}, u32[]{:S(2)}) collective-permute-start(bf16[128,1024]{1,0:T(8,128)(2,1)S(1)} %get-tuple-element.22), channel_id=1, source_target_pairs={{0,14},{2,0},{4,2},{6,4},{8,6},{10,8},{12,10},{14,12},{1,15},{3,1}... | collective-permute-start | bytes 786440 | tf_op jit(solution)/shard_map/ppermute | solution.py:311
  95.2 4.0 %collective-permute-done.2.arrived_ref = bf16[128,1024]{1,0:T(8,128)(2,1)S(1)} collective-permute-done((bf16[128,1024]{1,0:T(8,128)(2,1)S(1)}, bf16[128,1024]{1,0:T(8,128)(2,1)S(1)}, u32[]{:S(2)}, u32[]{:S(2)}) %collective-permute-start.2) | collective-permute-done | bytes 262176 | tf_op jit(solution)/shard_map/ppermute | solution.py:305
  99.2 0.1 shard_map.83
  99.3 4.6 %collective-permute-start.3 = (bf16[128,1024]{1,0:T(8,128)(2,1)S(1)}, bf16[128,1024]{1,0:T(8,128)(2,1)S(1)}, u32[]{:S(2)}, u32[]{:S(2)}) collective-permute-start(bf16[128,1024]{1,0:T(8,128)(2,1)S(1)} %shard_map.83), channel_id=1, source_target_pairs={{0,2},{2,4},{4,6},{6,8},{8,10},{10,12},{12,14},{14,0},{1,3},{3,5},... | collective-permute-start | bytes 786440 | tf_op jit(solution)/shard_map/ppermute | solution.py:305
  103.9 0.0 collective-permute-done.5.arrived_ref
  103.9 0.1 shard_map.85
  104.0 1.9 %collective-permute-start.6 = (bf16[128,1024]{1,0:T(8,128)(2,1)S(1)}, bf16[128,1024]{1,0:T(8,128)(2,1)S(1)}, u32[]{:S(2)}, u32[]{:S(2)}) collective-permute-start(bf16[128,1024]{1,0:T(8,128)(2,1)S(1)} %shard_map.85), channel_id=1, source_target_pairs={{0,14},{2,0},{4,2},{6,4},{8,6},{10,8},{12,10},{14,12},{1,15},{3,1}... | collective-permute-start | bytes 786440 | tf_op jit(solution)/shard_map/ppermute | solution.py:311
  105.9 2.6 %collective-permute-done.3.arrived_ref = bf16[128,1024]{1,0:T(8,128)(2,1)S(1)} collective-permute-done((bf16[128,1024]{1,0:T(8,128)(2,1)S(1)}, bf16[128,1024]{1,0:T(8,128)(2,1)S(1)}, u32[]{:S(2)}, u32[]{:S(2)}) %collective-permute-start.3) | collective-permute-done | bytes 262176 | tf_op jit(solution)/shard_map/ppermute | solution.py:305
  108.5 0.1 shard_map.84
  108.6 0.0 copy-start
  108.6 0.0 copy-start.1
  108.6 5.6 %collective-permute-start.4 = (bf16[128,1024]{1,0:T(8,128)(2,1)S(1)}, bf16[128,1024]{1,0:T(8,128)(2,1)S(1)}, u32[]{:S(2)}, u32[]{:S(2)}) collective-permute-start(bf16[128,1024]{1,0:T(8,128)(2,1)S(1)} %shard_map.84), channel_id=1, source_target_pairs={{0,2},{2,4},{4,6},{6,8},{8,10},{10,12},{12,14},{14,0},{1,3},{3,5},... | collective-permute-start | bytes 786440 | tf_op jit(solution)/shard_map/ppermute | solution.py:305
  114.2 0.0 collective-permute-done.6.arrived_ref
  114.2 0.1 shard_map.86
  114.3 1.9 %collective-permute-start.7 = (bf16[128,1024]{1,0:T(8,128)(2,1)S(1)}, bf16[128,1024]{1,0:T(8,128)(2,1)S(1)}, u32[]{:S(2)}, u32[]{:S(2)}) collective-permute-start(bf16[128,1024]{1,0:T(8,128)(2,1)S(1)} %shard_map.86), channel_id=1, source_target_pairs={{0,14},{2,0},{4,2},{6,4},{8,6},{10,8},{12,10},{14,12},{1,15},{3,1}... | collective-permute-start | bytes 786440 | tf_op jit(solution)/shard_map/ppermute | solution.py:311
  116.2 0.0 all-to-all-done.1
  116.3 1.3 %shard_map.81 = bf16[128,1024]{1,0:T(8,128)(2,1)} custom-call(s32[1,128]{1,0:T(1,128)S(1)} %bitcast.20, f32[1,128]{1,0:T(1,128)S(1)} %bitcast.22, bf16[1536,128]{1,0:T(8,128)(2,1)S(1)} %bitcast.18), custom_call_target="tpu_custom_call" | custom-call | flops 50331648 | bytes 655360 | tf_op jit(solution)/shard_map/pallas_call | solution.py:195
  117.5 0.6 collective-permute-done.4
  118.1 5.7 %collective-permute-done.7 = bf16[128,1024]{1,0:T(8,128)(2,1)S(1)} collective-permute-done((bf16[128,1024]{1,0:T(8,128)(2,1)S(1)}, bf16[128,1024]{1,0:T(8,128)(2,1)S(1)}, u32[]{:S(2)}, u32[]{:S(2)}) %collective-permute-start.7) | collective-permute-done | bytes 262176 | tf_op jit(solution)/shard_map/ppermute | solution.py:311
  123.8 0.8 fusion.2
  (3 shorter events, 0.0 us)
Async XLA Ops:
  67.5 4.8 %collective-permute-start = (bf16[3072,128]{1,0:T(8,128)(2,1)S(1)}, bf16[3072,128]{1,0:T(8,128)(2,1)S(1)}, u32[]{:S(2)}, u32[]{:S(2)}) collective-permute-start(bf16[3072,128]{1,0:T(8,128)(2,1)S(1)} %bitcast.15), channel_id=1, source_target_pairs={{0,1},{1,0},{2,3},{3,2},{4,5},{5,4},{6,7},{7,6},{8,9},{9,8},{10,11... | collective-permute-start | bytes 2359304 | tf_op jit(solution)/shard_map/ppermute | solution.py:241
  76.1 13.2 %collective-permute-start.1 = (bf16[128,1024]{1,0:T(8,128)(2,1)S(1)}, bf16[128,1024]{1,0:T(8,128)(2,1)S(1)}, u32[]{:S(2)}, u32[]{:S(2)}) collective-permute-start(bf16[128,1024]{1,0:T(8,128)(2,1)S(1)} %get-tuple-element.18), channel_id=1, source_target_pairs={{0,2},{2,4},{4,6},{6,8},{8,10},{10,12},{12,14},{14,0},{1,3},{3,5},... | collective-permute-start | bytes 786440 | tf_op jit(solution)/shard_map/ppermute | solution.py:305
  82.6 33.6 %all-to-all-start.1 = ((bf16[64,24,128]{2,1,0:T(8,128)(2,1)}), bf16[64,24,128]{2,1,0:T(8,128)(2,1)S(1)}, u32[]{:S(2)}, u32[]{:S(2)}) async-start(bf16[64,24,128]{2,1,0:T(8,128)(2,1)} %bitcast.8), calls=%async_computation.1 | async-start | bytes 786432 | tf_op jit(solution)/shard_map/all_to_all | solution.py:314
  89.4 9.8 %collective-permute-start.2 = (bf16[128,1024]{1,0:T(8,128)(2,1)S(1)}, bf16[128,1024]{1,0:T(8,128)(2,1)S(1)}, u32[]{:S(2)}, u32[]{:S(2)}) collective-permute-start(bf16[128,1024]{1,0:T(8,128)(2,1)S(1)} %shard_map.82), channel_id=1, source_target_pairs={{0,2},{2,4},{4,6},{6,8},{8,10},{10,12},{12,14},{14,0},{1,3},{3,5},... | collective-permute-start | bytes 786440 | tf_op jit(solution)/shard_map/ppermute | solution.py:305
  92.7 11.2 %collective-permute-start.5 = (bf16[128,1024]{1,0:T(8,128)(2,1)S(1)}, bf16[128,1024]{1,0:T(8,128)(2,1)S(1)}, u32[]{:S(2)}, u32[]{:S(2)}) collective-permute-start(bf16[128,1024]{1,0:T(8,128)(2,1)S(1)} %get-tuple-element.22), channel_id=1, source_target_pairs={{0,14},{2,0},{4,2},{6,4},{8,6},{10,8},{12,10},{14,12},{1,15},{3,1}... | collective-permute-start | bytes 786440 | tf_op jit(solution)/shard_map/ppermute | solution.py:311
  99.3 9.3 %collective-permute-start.3 = (bf16[128,1024]{1,0:T(8,128)(2,1)S(1)}, bf16[128,1024]{1,0:T(8,128)(2,1)S(1)}, u32[]{:S(2)}, u32[]{:S(2)}) collective-permute-start(bf16[128,1024]{1,0:T(8,128)(2,1)S(1)} %shard_map.83), channel_id=1, source_target_pairs={{0,2},{2,4},{4,6},{6,8},{8,10},{10,12},{12,14},{14,0},{1,3},{3,5},... | collective-permute-start | bytes 786440 | tf_op jit(solution)/shard_map/ppermute | solution.py:305
  104.0 10.2 %collective-permute-start.6 = (bf16[128,1024]{1,0:T(8,128)(2,1)S(1)}, bf16[128,1024]{1,0:T(8,128)(2,1)S(1)}, u32[]{:S(2)}, u32[]{:S(2)}) collective-permute-start(bf16[128,1024]{1,0:T(8,128)(2,1)S(1)} %shard_map.85), channel_id=1, source_target_pairs={{0,14},{2,0},{4,2},{6,4},{8,6},{10,8},{12,10},{14,12},{1,15},{3,1}... | collective-permute-start | bytes 786440 | tf_op jit(solution)/shard_map/ppermute | solution.py:311
  108.6 7.7 %copy-start = (s32[128,1]{0,1:T(1,128)S(1)}, s32[128,1]{0,1:T(1,128)}, u32[]{:S(2)}) copy-start(s32[128,1]{0,1:T(1,128)} %param.8) | copy-start | bytes 1540
  108.6 7.7 %copy-start.1 = (f32[128,1]{0,1:T(1,128)S(1)}, f32[128,1]{0,1:T(1,128)}, u32[]{:S(2)}) copy-start(f32[128,1]{0,1:T(1,128)} %param.9) | copy-start | bytes 1540
  108.6 9.5 %collective-permute-start.4 = (bf16[128,1024]{1,0:T(8,128)(2,1)S(1)}, bf16[128,1024]{1,0:T(8,128)(2,1)S(1)}, u32[]{:S(2)}, u32[]{:S(2)}) collective-permute-start(bf16[128,1024]{1,0:T(8,128)(2,1)S(1)} %shard_map.84), channel_id=1, source_target_pairs={{0,2},{2,4},{4,6},{6,8},{8,10},{10,12},{12,14},{14,0},{1,3},{3,5},... | collective-permute-start | bytes 786440 | tf_op jit(solution)/shard_map/ppermute | solution.py:305
  114.3 9.5 %collective-permute-start.7 = (bf16[128,1024]{1,0:T(8,128)(2,1)S(1)}, bf16[128,1024]{1,0:T(8,128)(2,1)S(1)}, u32[]{:S(2)}, u32[]{:S(2)}) collective-permute-start(bf16[128,1024]{1,0:T(8,128)(2,1)S(1)} %shard_map.86), channel_id=1, source_target_pairs={{0,14},{2,0},{4,2},{6,4},{8,6},{10,8},{12,10},{14,12},{1,15},{3,1}... | collective-permute-start | bytes 786440 | tf_op jit(solution)/shard_map/ppermute | solution.py:311

commit v6 on v5

--- a/solution.py
+++ b/solution.py
@@ -124,7 +124,8 @@
     for j in range(0, len(offsets), 4):
         columns = []
         for offset in offsets[j : j + 4]:
-            y = lax.rem(place_ref[0] + offset, place_ref[2])
+            turn = jnp.where(place_ref[1] == 0, offset, place_ref[2] - offset)
+            y = lax.rem(place_ref[0] + turn, place_ref[2])
             columns.append(pl.ds(pl.multiple_of((CORES * y + place_ref[1]) * LANES, LANES), LANES))
         at = pl.ds(j * LANES, 4 * LANES)
         weight = jnp.concatenate([up_ref[:, column] for column in columns], axis=1)
@@ -288,8 +289,14 @@
         2 * slots * width * hidden_width,
         2 * width * hidden_width + 4 * slots * width,
     )(hidden, down)
-    after = [(i, (i + 1) % ring) for i in range(ring)]
-    before = [(i, (i - 1) % ring) for i in range(ring)]
+    after, before = (
+        [
+            (i * CORES + core, (i + (step if core == 0 else -step)) % ring * CORES + core)
+            for i in range(ring)
+            for core in range(CORES)
+        ]
+        for step in (1, -1)
+    )
 
     def add(arrived, offset):
         return call(
@@ -302,13 +309,13 @@
 
     total = parts[rest.index(0)]
     for hop in range(far):
-        upward = lax.ppermute(upward, "y", after)
+        upward = lax.ppermute(upward, ("y", "core"), after)
         if hop == 0:
             upward, downward = lax.optimization_barrier((upward, downward))
         if hop < far - 1:
             upward = add(upward, far - 1 - hop)
     for hop in range(near):
-        downward = lax.ppermute(downward, "y", before)
+        downward = lax.ppermute(downward, ("y", "core"), before)
         if hop < near - 1:
             downward = add(downward, ring - near + 1 + hop)
     returned = lax.all_to_all(

time: 125 us -> 127 us (1.016)
  waiting for transfers between devices: 12.8 us -> 14.3 us
    ppermute x7, waiting for transfers between devices: 12.8 us -> 14.3 us  [the longest x4 10.3 us: on_device(): upward = lax.ppermute(upward, ('y', 'core'), after)]
where the time goes in v6:
time: 127 us; the launch traced here: 126 us
  blocking collectives  65 us (51%)
  starting transfers between devices  33.3 us (26%)
  waiting for transfers between devices  14.3 us (11%)
  Pallas kernels  11.8 us (9%)
    all_to_all x1, blocking collectives, on_device(): lax.all_to_all(sent.reshape(experts, -1, LANES), 'expert', split_axis=0,...  65 us
    ppermute x4, starting transfers between devices, on_device(): upward = lax.ppermute(upward, ('y', 'core'), after)  17.6 us
    pallas_call x10, Pallas kernels, run(): pl.pallas_call(kernel, out_shape=out_shape, in_specs=[spec(i) for i in ra...  11.8 us
    ppermute x4, waiting for transfers between devices, on_device(): upward = lax.ppermute(upward, ('y', 'core'), after)  10.3 us
    ppermute x3, starting transfers between devices, on_device(): downward = lax.ppermute(downward, ('y', 'core'), before)  7.11 us
    all_to_all x1, starting transfers between devices, on_device(): lax.all_to_all(out.reshape(experts, -1, LANES), 'expert', split_axis=0, c...  6.65 us
    ppermute x3, waiting for transfers between devices, on_device(): downward = lax.ppermute(downward, ('y', 'core'), before)  4.06 us
  transfers between devices with their start and end apart: 9, of which 4 were waited for; matrix products, arithmetic and copies ran while one was open for 0% of the time, Pallas kernels for 5%

profile of v6, /device:TPU:30, one launch (start us, length us, event | category | flops | bytes accessed | tf_op | source)
XLA Modules:
  0.0 126.2 jit_solution(14013813529496844517)
XLA Ops:
  0.6 1.8 %shard_map.77 = bf16[3072,128]{1,0:T(8,128)(2,1)S(1)} custom-call(s32[1,128]{1,0:T(1,128)} %bitcast.19, f32[1,128]{1,0:T(1,128)} %bitcast.21, bf16[128,1024]{1,0:T(8,128)(2,1)} %latent_hbm.1, bf16[128,1024]{1,0:T(8,128)(2,1)} %cot_hbm.1), custom_call_target="tpu_custom_call" | custom-call | flops 100663296 | bytes 1310720 | tf_op jit(solution)/shard_map/pallas_call | solution.py:196
  2.5 65.0 %all_to_all.10 = bf16[64,48,128]{2,1,0:T(8,128)(2,1)S(1)} all-to-all(bf16[64,48,128]{2,1,0:T(8,128)(2,1)S(1)} %bitcast.17), channel_id=1, replica_groups=mesh['expert'=64,'y'=8,'core'=2] {'expert'}, dimensions={0} | all-to-all | bytes 1572864 | tf_op jit(solution)/shard_map/all_to_all | solution.py:239
  67.5 1.9 %collective-permute-start = (bf16[3072,128]{1,0:T(8,128)(2,1)S(1)}, bf16[3072,128]{1,0:T(8,128)(2,1)S(1)}, u32[]{:S(2)}, u32[]{:S(2)}) collective-permute-start(bf16[3072,128]{1,0:T(8,128)(2,1)S(1)} %bitcast.15), channel_id=1, source_target_pairs={{0,1},{1,0},{2,3},{3,2},{4,5},{5,4},{6,7},{7,6},{8,9},{9,8},{10,11... | collective-permute-start | bytes 2359304 | tf_op jit(solution)/shard_map/ppermute | solution.py:242
  69.4 0.1 pad_add_fusion.place_ref
  69.5 2.8 %shard_map.78 = (bf16[192,2048]{1,0:T(8,128)(2,1)S(1)}, bf16[192,1024]{1,0:T(8,128)(2,1)S(1)}, bf16[1024,2048]{1,0:T(8,128)(2,1)S(1)}) custom-call(bf16[3072,128]{1,0:T(8,128)(2,1)S(1)} %bitcast.16, bf16[1024,2048]{1,0:T(8,128)(2,1)} %bitcast.23), custom_call_target="tpu_custom_call" | custom-call | flops 805306368 | bytes 6160384 | tf_op jit(solution)/shard_map/pallas_call | solution.py:196
  72.3 0.0 collective-permute-done.other_ref
  72.3 3.7 %shard_map.79 = (bf16[128,1024]{1,0:T(8,128)(2,1)S(1)}, bf16[128,1024]{1,0:T(8,128)(2,1)S(1)}, bf16[6,128,1024]{2,1,0:T(8,128)(2,1)S(1)}, bf16[2048,1024]{1,0:T(8,128)(2,1)S(1)}) custom-call(s32[3]{0:T(128)S(1)} %pad_add_fusion.place_ref, bf16[192,2048]{1,0:T(8,128)(2,1)S(1)} %get-tuple-element.14.hidden_ref, ...), custom_call_target="tpu_custom_call" | custom-call | flops 1207959552 | bytes 5767168 | tf_op jit(solution)/shard_map/pallas_call | solution.py:196
  76.1 4.7 %collective-permute-start.1 = (bf16[128,1024]{1,0:T(8,128)(2,1)S(1)}, bf16[128,1024]{1,0:T(8,128)(2,1)S(1)}, u32[]{:S(2)}, u32[]{:S(2)}) collective-permute-start(bf16[128,1024]{1,0:T(8,128)(2,1)S(1)} %get-tuple-element.18), channel_id=1, source_target_pairs={{0,2},{1,15},{2,4},{3,1},{4,6},{5,3},{6,8},{7,5},{8,10},{9,7},{10,... | collective-permute-start | bytes 786440 | tf_op jit(solution)/shard_map/ppermute | solution.py:312
  80.8 1.8 %shard_map.80 = bf16[1536,128]{1,0:T(8,128)(2,1)} custom-call(bf16[192,2048]{1,0:T(8,128)(2,1)S(1)} %get-tuple-element.14.hidden_ref, bf16[2048,1024]{1,0:T(8,128)(2,1)S(1)} %get-tuple-element.17.down_ref), custom_call_target="tpu_custom_call" | custom-call | flops 805306368 | bytes 4980736 | tf_op jit(solution)/shard_map/pallas_call | solution.py:196
  82.6 6.6 %all-to-all-start.1 = ((bf16[64,24,128]{2,1,0:T(8,128)(2,1)}), bf16[64,24,128]{2,1,0:T(8,128)(2,1)S(1)}, u32[]{:S(2)}, u32[]{:S(2)}) async-start(bf16[64,24,128]{2,1,0:T(8,128)(2,1)} %bitcast.8), calls=%async_computation.1 | async-start | bytes 786432 | tf_op jit(solution)/shard_map/all_to_all | solution.py:321
  89.3 0.0 collective-permute-done.1.arrived_ref
  89.3 0.1 shard_map.82
  89.4 2.6 %collective-permute-start.2 = (bf16[128,1024]{1,0:T(8,128)(2,1)S(1)}, bf16[128,1024]{1,0:T(8,128)(2,1)S(1)}, u32[]{:S(2)}, u32[]{:S(2)}) collective-permute-start(bf16[128,1024]{1,0:T(8,128)(2,1)S(1)} %shard_map.82), channel_id=1, source_target_pairs={{0,2},{1,15},{2,4},{3,1},{4,6},{5,3},{6,8},{7,5},{8,10},{9,7},{10,... | collective-permute-start | bytes 786440 | tf_op jit(solution)/shard_map/ppermute | solution.py:312
  91.9 3.3 %collective-permute-start.5 = (bf16[128,1024]{1,0:T(8,128)(2,1)S(1)}, bf16[128,1024]{1,0:T(8,128)(2,1)S(1)}, u32[]{:S(2)}, u32[]{:S(2)}) collective-permute-start(bf16[128,1024]{1,0:T(8,128)(2,1)S(1)} %get-tuple-element.22), channel_id=1, source_target_pairs={{0,14},{1,3},{2,0},{3,5},{4,2},{5,7},{6,4},{7,9},{8,6},{9,11},{10,... | collective-permute-start | bytes 786440 | tf_op jit(solution)/shard_map/ppermute | solution.py:318
  95.2 3.7 %collective-permute-done.2.arrived_ref = bf16[128,1024]{1,0:T(8,128)(2,1)S(1)} collective-permute-done((bf16[128,1024]{1,0:T(8,128)(2,1)S(1)}, bf16[128,1024]{1,0:T(8,128)(2,1)S(1)}, u32[]{:S(2)}, u32[]{:S(2)}) %collective-permute-start.2) | collective-permute-done | bytes 262176 | tf_op jit(solution)/shard_map/ppermute | solution.py:312
  98.9 0.1 shard_map.83
  99.0 4.8 %collective-permute-start.3 = (bf16[128,1024]{1,0:T(8,128)(2,1)S(1)}, bf16[128,1024]{1,0:T(8,128)(2,1)S(1)}, u32[]{:S(2)}, u32[]{:S(2)}) collective-permute-start(bf16[128,1024]{1,0:T(8,128)(2,1)S(1)} %shard_map.83), channel_id=1, source_target_pairs={{0,2},{1,15},{2,4},{3,1},{4,6},{5,3},{6,8},{7,5},{8,10},{9,7},{10,... | collective-permute-start | bytes 786440 | tf_op jit(solution)/shard_map/ppermute | solution.py:312
  103.7 0.0 collective-permute-done.5.arrived_ref
  103.7 0.1 shard_map.85
  103.8 1.9 %collective-permute-start.6 = (bf16[128,1024]{1,0:T(8,128)(2,1)S(1)}, bf16[128,1024]{1,0:T(8,128)(2,1)S(1)}, u32[]{:S(2)}, u32[]{:S(2)}) collective-permute-start(bf16[128,1024]{1,0:T(8,128)(2,1)S(1)} %shard_map.85), channel_id=1, source_target_pairs={{0,14},{1,3},{2,0},{3,5},{4,2},{5,7},{6,4},{7,9},{8,6},{9,11},{10,... | collective-permute-start | bytes 786440 | tf_op jit(solution)/shard_map/ppermute | solution.py:318
  105.7 4.4 %collective-permute-done.3.arrived_ref = bf16[128,1024]{1,0:T(8,128)(2,1)S(1)} collective-permute-done((bf16[128,1024]{1,0:T(8,128)(2,1)S(1)}, bf16[128,1024]{1,0:T(8,128)(2,1)S(1)}, u32[]{:S(2)}, u32[]{:S(2)}) %collective-permute-start.3) | collective-permute-done | bytes 262176 | tf_op jit(solution)/shard_map/ppermute | solution.py:312
  110.1 0.1 shard_map.84
  110.2 0.0 copy-start
  110.2 0.0 copy-start.1
  110.2 5.6 %collective-permute-start.4 = (bf16[128,1024]{1,0:T(8,128)(2,1)S(1)}, bf16[128,1024]{1,0:T(8,128)(2,1)S(1)}, u32[]{:S(2)}, u32[]{:S(2)}) collective-permute-start(bf16[128,1024]{1,0:T(8,128)(2,1)S(1)} %shard_map.84), channel_id=1, source_target_pairs={{0,2},{1,15},{2,4},{3,1},{4,6},{5,3},{6,8},{7,5},{8,10},{9,7},{10,... | collective-permute-start | bytes 786440 | tf_op jit(solution)/shard_map/ppermute | solution.py:312
  115.8 0.0 collective-permute-done.6.arrived_ref
  115.8 0.1 shard_map.86
  115.9 1.9 %collective-permute-start.7 = (bf16[128,1024]{1,0:T(8,128)(2,1)S(1)}, bf16[128,1024]{1,0:T(8,128)(2,1)S(1)}, u32[]{:S(2)}, u32[]{:S(2)}) collective-permute-start(bf16[128,1024]{1,0:T(8,128)(2,1)S(1)} %shard_map.86), channel_id=1, source_target_pairs={{0,14},{1,3},{2,0},{3,5},{4,2},{5,7},{6,4},{7,9},{8,6},{9,11},{10,... | collective-permute-start | bytes 786440 | tf_op jit(solution)/shard_map/ppermute | solution.py:318
  117.9 1.3 shard_map.81
  119.1 2.2 %collective-permute-done.4 = bf16[128,1024]{1,0:T(8,128)(2,1)S(1)} collective-permute-done((bf16[128,1024]{1,0:T(8,128)(2,1)S(1)}, bf16[128,1024]{1,0:T(8,128)(2,1)S(1)}, u32[]{:S(2)}, u32[]{:S(2)}) %collective-permute-start.4) | collective-permute-done | bytes 262176 | tf_op jit(solution)/shard_map/ppermute | solution.py:312
  121.3 4.1 %collective-permute-done.7 = bf16[128,1024]{1,0:T(8,128)(2,1)S(1)} collective-permute-done((bf16[128,1024]{1,0:T(8,128)(2,1)S(1)}, bf16[128,1024]{1,0:T(8,128)(2,1)S(1)}, u32[]{:S(2)}, u32[]{:S(2)}) %collective-permute-start.7) | collective-permute-done | bytes 262176 | tf_op jit(solution)/shard_map/ppermute | solution.py:318
  125.4 0.8 fusion.2
  (3 shorter events, 0.0 us)
Async XLA Ops:
  67.5 4.8 %collective-permute-start = (bf16[3072,128]{1,0:T(8,128)(2,1)S(1)}, bf16[3072,128]{1,0:T(8,128)(2,1)S(1)}, u32[]{:S(2)}, u32[]{:S(2)}) collective-permute-start(bf16[3072,128]{1,0:T(8,128)(2,1)S(1)} %bitcast.15), channel_id=1, source_target_pairs={{0,1},{1,0},{2,3},{3,2},{4,5},{5,4},{6,7},{7,6},{8,9},{9,8},{10,11... | collective-permute-start | bytes 2359304 | tf_op jit(solution)/shard_map/ppermute | solution.py:242
  76.1 13.2 %collective-permute-start.1 = (bf16[128,1024]{1,0:T(8,128)(2,1)S(1)}, bf16[128,1024]{1,0:T(8,128)(2,1)S(1)}, u32[]{:S(2)}, u32[]{:S(2)}) collective-permute-start(bf16[128,1024]{1,0:T(8,128)(2,1)S(1)} %get-tuple-element.18), channel_id=1, source_target_pairs={{0,2},{1,15},{2,4},{3,1},{4,6},{5,3},{6,8},{7,5},{8,10},{9,7},{10,... | collective-permute-start | bytes 786440 | tf_op jit(solution)/shard_map/ppermute | solution.py:312
  82.6 35.2 %all-to-all-start.1 = ((bf16[64,24,128]{2,1,0:T(8,128)(2,1)}), bf16[64,24,128]{2,1,0:T(8,128)(2,1)S(1)}, u32[]{:S(2)}, u32[]{:S(2)}) async-start(bf16[64,24,128]{2,1,0:T(8,128)(2,1)} %bitcast.8), calls=%async_computation.1 | async-start | bytes 786432 | tf_op jit(solution)/shard_map/all_to_all | solution.py:321
  89.4 9.5 %collective-permute-start.2 = (bf16[128,1024]{1,0:T(8,128)(2,1)S(1)}, bf16[128,1024]{1,0:T(8,128)(2,1)S(1)}, u32[]{:S(2)}, u32[]{:S(2)}) collective-permute-start(bf16[128,1024]{1,0:T(8,128)(2,1)S(1)} %shard_map.82), channel_id=1, source_target_pairs={{0,2},{1,15},{2,4},{3,1},{4,6},{5,3},{6,8},{7,5},{8,10},{9,7},{10,... | collective-permute-start | bytes 786440 | tf_op jit(solution)/shard_map/ppermute | solution.py:312
  91.9 11.8 %collective-permute-start.5 = (bf16[128,1024]{1,0:T(8,128)(2,1)S(1)}, bf16[128,1024]{1,0:T(8,128)(2,1)S(1)}, u32[]{:S(2)}, u32[]{:S(2)}) collective-permute-start(bf16[128,1024]{1,0:T(8,128)(2,1)S(1)} %get-tuple-element.22), channel_id=1, source_target_pairs={{0,14},{1,3},{2,0},{3,5},{4,2},{5,7},{6,4},{7,9},{8,6},{9,11},{10,... | collective-permute-start | bytes 786440 | tf_op jit(solution)/shard_map/ppermute | solution.py:318
  99.0 11.1 %collective-permute-start.3 = (bf16[128,1024]{1,0:T(8,128)(2,1)S(1)}, bf16[128,1024]{1,0:T(8,128)(2,1)S(1)}, u32[]{:S(2)}, u32[]{:S(2)}) collective-permute-start(bf16[128,1024]{1,0:T(8,128)(2,1)S(1)} %shard_map.83), channel_id=1, source_target_pairs={{0,2},{1,15},{2,4},{3,1},{4,6},{5,3},{6,8},{7,5},{8,10},{9,7},{10,... | collective-permute-start | bytes 786440 | tf_op jit(solution)/shard_map/ppermute | solution.py:312
  103.8 12.0 %collective-permute-start.6 = (bf16[128,1024]{1,0:T(8,128)(2,1)S(1)}, bf16[128,1024]{1,0:T(8,128)(2,1)S(1)}, u32[]{:S(2)}, u32[]{:S(2)}) collective-permute-start(bf16[128,1024]{1,0:T(8,128)(2,1)S(1)} %shard_map.85), channel_id=1, source_target_pairs={{0,14},{1,3},{2,0},{3,5},{4,2},{5,7},{6,4},{7,9},{8,6},{9,11},{10,... | collective-permute-start | bytes 786440 | tf_op jit(solution)/shard_map/ppermute | solution.py:318
  110.2 7.7 %copy-start = (s32[128,1]{0,1:T(1,128)S(1)}, s32[128,1]{0,1:T(1,128)}, u32[]{:S(2)}) copy-start(s32[128,1]{0,1:T(1,128)} %param.8) | copy-start | bytes 1540
  110.2 7.7 %copy-start.1 = (f32[128,1]{0,1:T(1,128)S(1)}, f32[128,1]{0,1:T(1,128)}, u32[]{:S(2)}) copy-start(f32[128,1]{0,1:T(1,128)} %param.9) | copy-start | bytes 1540
  110.2 11.1 %collective-permute-start.4 = (bf16[128,1024]{1,0:T(8,128)(2,1)S(1)}, bf16[128,1024]{1,0:T(8,128)(2,1)S(1)}, u32[]{:S(2)}, u32[]{:S(2)}) collective-permute-start(bf16[128,1024]{1,0:T(8,128)(2,1)S(1)} %shard_map.84), channel_id=1, source_target_pairs={{0,2},{1,15},{2,4},{3,1},{4,6},{5,3},{6,8},{7,5},{8,10},{9,7},{10,... | collective-permute-start | bytes 786440 | tf_op jit(solution)/shard_map/ppermute | solution.py:312
  115.9 9.5 %collective-permute-start.7 = (bf16[128,1024]{1,0:T(8,128)(2,1)S(1)}, bf16[128,1024]{1,0:T(8,128)(2,1)S(1)}, u32[]{:S(2)}, u32[]{:S(2)}) collective-permute-start(bf16[128,1024]{1,0:T(8,128)(2,1)S(1)} %shard_map.86), channel_id=1, source_target_pairs={{0,14},{1,3},{2,0},{3,5},{4,2},{5,7},{6,4},{7,9},{8,6},{9,11},{10,... | collective-permute-start | bytes 786440 | tf_op jit(solution)/shard_map/ppermute | solution.py:318

commit v7 on v6

--- a/solution.py
+++ b/solution.py
@@ -310,12 +310,10 @@
     total = parts[rest.index(0)]
     for hop in range(far):
         upward = lax.ppermute(upward, ("y", "core"), after)
-        if hop == 0:
-            upward, downward = lax.optimization_barrier((upward, downward))
+        if hop < near:
+            downward = lax.ppermute(downward, ("y", "core"), before)
         if hop < far - 1:
             upward = add(upward, far - 1 - hop)
-    for hop in range(near):
-        downward = lax.ppermute(downward, ("y", "core"), before)
         if hop < near - 1:
             downward = add(downward, ring - near + 1 + hop)
     returned = lax.all_to_all(

time: 127 us -> 126 us (level)
  the two profiles are of different devices: /device:TPU:30 before, /device:TPU:38 now
where the time goes in v7:
time: 126 us
  blocking collectives  65 us (52%)
  starting transfers between devices  32.6 us (26%)
  waiting for transfers between devices  14.7 us (12%)
  Pallas kernels  11.8 us (9%)
    all_to_all x1, blocking collectives, on_device(): lax.all_to_all(sent.reshape(experts, -1, LANES), 'expert', split_axis=0,...  65 us
    ppermute x3, starting transfers between devices, on_device(): downward = lax.ppermute(downward, ('y', 'core'), before)  15.7 us
    pallas_call x10, Pallas kernels, run(): pl.pallas_call(kernel, out_shape=out_shape, in_specs=[spec(i) for i in ra...  11.8 us
    ppermute x3, waiting for transfers between devices, on_device(): downward = lax.ppermute(downward, ('y', 'core'), before)  11 us
    ppermute x4, starting transfers between devices, on_device(): upward = lax.ppermute(upward, ('y', 'core'), after)  8.34 us
    all_to_all x1, starting transfers between devices, on_device(): lax.all_to_all(out.reshape(experts, -1, LANES), 'expert', split_axis=0, c...  6.64 us
    ppermute x4, waiting for transfers between devices, on_device(): upward = lax.ppermute(upward, ('y', 'core'), after)  3.74 us
  transfers between devices with their start and end apart: 9, of which 4 were waited for; matrix products, arithmetic and copies ran while one was open for 0% of the time, Pallas kernels for 5%

profile of v7, /device:TPU:38, one launch (start us, length us, event | category | flops | bytes accessed | tf_op | source)
XLA Modules:
  0.0 125.9 jit_solution(5954772825445546685)
XLA Ops:
  0.6 1.8 %shard_map.77 = bf16[3072,128]{1,0:T(8,128)(2,1)S(1)} custom-call(s32[1,128]{1,0:T(1,128)} %bitcast.19, f32[1,128]{1,0:T(1,128)} %bitcast.21, bf16[128,1024]{1,0:T(8,128)(2,1)} %latent_hbm.1, bf16[128,1024]{1,0:T(8,128)(2,1)} %cot_hbm.1), custom_call_target="tpu_custom_call" | custom-call | flops 100663296 | bytes 1310720 | tf_op jit(solution)/shard_map/pallas_call | solution.py:196
  2.5 65.0 %all_to_all.10 = bf16[64,48,128]{2,1,0:T(8,128)(2,1)S(1)} all-to-all(bf16[64,48,128]{2,1,0:T(8,128)(2,1)S(1)} %bitcast.17), channel_id=1, replica_groups=mesh['expert'=64,'y'=8,'core'=2] {'expert'}, dimensions={0} | all-to-all | bytes 1572864 | tf_op jit(solution)/shard_map/all_to_all | solution.py:239
  67.5 1.9 %collective-permute-start = (bf16[3072,128]{1,0:T(8,128)(2,1)S(1)}, bf16[3072,128]{1,0:T(8,128)(2,1)S(1)}, u32[]{:S(2)}, u32[]{:S(2)}) collective-permute-start(bf16[3072,128]{1,0:T(8,128)(2,1)S(1)} %bitcast.15), channel_id=1, source_target_pairs={{0,1},{1,0},{2,3},{3,2},{4,5},{5,4},{6,7},{7,6},{8,9},{9,8},{10,11... | collective-permute-start | bytes 2359304 | tf_op jit(solution)/shard_map/ppermute | solution.py:242
  69.4 0.1 pad_add_fusion.place_ref
  69.5 2.8 %shard_map.78 = (bf16[192,2048]{1,0:T(8,128)(2,1)S(1)}, bf16[192,1024]{1,0:T(8,128)(2,1)S(1)}, bf16[1024,2048]{1,0:T(8,128)(2,1)S(1)}) custom-call(bf16[3072,128]{1,0:T(8,128)(2,1)S(1)} %bitcast.16, bf16[1024,2048]{1,0:T(8,128)(2,1)} %bitcast.23), custom_call_target="tpu_custom_call" | custom-call | flops 805306368 | bytes 6160384 | tf_op jit(solution)/shard_map/pallas_call | solution.py:196
  72.3 0.0 collective-permute-done.other_ref
  72.3 3.7 %shard_map.79 = (bf16[128,1024]{1,0:T(8,128)(2,1)S(1)}, bf16[128,1024]{1,0:T(8,128)(2,1)S(1)}, bf16[6,128,1024]{2,1,0:T(8,128)(2,1)S(1)}, bf16[2048,1024]{1,0:T(8,128)(2,1)S(1)}) custom-call(s32[3]{0:T(128)S(1)} %pad_add_fusion.place_ref, bf16[192,2048]{1,0:T(8,128)(2,1)S(1)} %get-tuple-element.12.hidden_ref, ...), custom_call_target="tpu_custom_call" | custom-call | flops 1207959552 | bytes 5767168 | tf_op jit(solution)/shard_map/pallas_call | solution.py:196
  76.1 2.6 %collective-permute-start.1 = (bf16[128,1024]{1,0:T(8,128)(2,1)S(1)}, bf16[128,1024]{1,0:T(8,128)(2,1)S(1)}, u32[]{:S(2)}, u32[]{:S(2)}) collective-permute-start(bf16[128,1024]{1,0:T(8,128)(2,1)S(1)} %get-tuple-element.16), channel_id=1, source_target_pairs={{0,2},{1,15},{2,4},{3,1},{4,6},{5,3},{6,8},{7,5},{8,10},{9,7},{10,... | collective-permute-start | bytes 786440 | tf_op jit(solution)/shard_map/ppermute | solution.py:312
  78.7 1.8 %shard_map.80 = bf16[1536,128]{1,0:T(8,128)(2,1)} custom-call(bf16[192,2048]{1,0:T(8,128)(2,1)S(1)} %get-tuple-element.12.hidden_ref, bf16[2048,1024]{1,0:T(8,128)(2,1)S(1)} %get-tuple-element.15.down_ref), custom_call_target="tpu_custom_call" | custom-call | flops 805306368 | bytes 4980736 | tf_op jit(solution)/shard_map/pallas_call | solution.py:196
  80.5 6.6 %all-to-all-start.1 = ((bf16[64,24,128]{2,1,0:T(8,128)(2,1)}), bf16[64,24,128]{2,1,0:T(8,128)(2,1)S(1)}, u32[]{:S(2)}, u32[]{:S(2)}) async-start(bf16[64,24,128]{2,1,0:T(8,128)(2,1)} %bitcast.8), calls=%async_computation.1 | async-start | bytes 786432 | tf_op jit(solution)/shard_map/all_to_all | solution.py:319
  87.2 4.5 %collective-permute-start.5 = (bf16[128,1024]{1,0:T(8,128)(2,1)S(1)}, bf16[128,1024]{1,0:T(8,128)(2,1)S(1)}, u32[]{:S(2)}, u32[]{:S(2)}) collective-permute-start(bf16[128,1024]{1,0:T(8,128)(2,1)S(1)} %get-tuple-element.18), channel_id=1, source_target_pairs={{0,14},{1,3},{2,0},{3,5},{4,2},{5,7},{6,4},{7,9},{8,6},{9,11},{10,... | collective-permute-start | bytes 786440 | tf_op jit(solution)/shard_map/ppermute | solution.py:314
  91.6 0.0 collective-permute-done.1.arrived_ref
  91.7 0.1 shard_map.82
  91.7 1.9 %collective-permute-start.2 = (bf16[128,1024]{1,0:T(8,128)(2,1)S(1)}, bf16[128,1024]{1,0:T(8,128)(2,1)S(1)}, u32[]{:S(2)}, u32[]{:S(2)}) collective-permute-start(bf16[128,1024]{1,0:T(8,128)(2,1)S(1)} %shard_map.82), channel_id=1, source_target_pairs={{0,2},{1,15},{2,4},{3,1},{4,6},{5,3},{6,8},{7,5},{8,10},{9,7},{10,... | collective-permute-start | bytes 786440 | tf_op jit(solution)/shard_map/ppermute | solution.py:312
  93.7 3.8 %collective-permute-done.5.arrived_ref = bf16[128,1024]{1,0:T(8,128)(2,1)S(1)} collective-permute-done((bf16[128,1024]{1,0:T(8,128)(2,1)S(1)}, bf16[128,1024]{1,0:T(8,128)(2,1)S(1)}, u32[]{:S(2)}, u32[]{:S(2)}) %collective-permute-start.5) | collective-permute-done | bytes 262176 | tf_op jit(solution)/shard_map/ppermute | solution.py:314
  97.4 0.1 shard_map.85
  97.5 5.6 %collective-permute-start.6 = (bf16[128,1024]{1,0:T(8,128)(2,1)S(1)}, bf16[128,1024]{1,0:T(8,128)(2,1)S(1)}, u32[]{:S(2)}, u32[]{:S(2)}) collective-permute-start(bf16[128,1024]{1,0:T(8,128)(2,1)S(1)} %shard_map.85), channel_id=1, source_target_pairs={{0,14},{1,3},{2,0},{3,5},{4,2},{5,7},{6,4},{7,9},{8,6},{9,11},{10,... | collective-permute-start | bytes 786440 | tf_op jit(solution)/shard_map/ppermute | solution.py:314
  103.1 0.1 shard_map.83
  103.2 1.9 %collective-permute-start.3 = (bf16[128,1024]{1,0:T(8,128)(2,1)S(1)}, bf16[128,1024]{1,0:T(8,128)(2,1)S(1)}, u32[]{:S(2)}, u32[]{:S(2)}) collective-permute-start(bf16[128,1024]{1,0:T(8,128)(2,1)S(1)} %shard_map.83), channel_id=1, source_target_pairs={{0,2},{1,15},{2,4},{3,1},{4,6},{5,3},{6,8},{7,5},{8,10},{9,7},{10,... | collective-permute-start | bytes 786440 | tf_op jit(solution)/shard_map/ppermute | solution.py:312
  105.1 4.6 %collective-permute-done.6.arrived_ref = bf16[128,1024]{1,0:T(8,128)(2,1)S(1)} collective-permute-done((bf16[128,1024]{1,0:T(8,128)(2,1)S(1)}, bf16[128,1024]{1,0:T(8,128)(2,1)S(1)}, u32[]{:S(2)}, u32[]{:S(2)}) %collective-permute-start.6) | collective-permute-done | bytes 262176 | tf_op jit(solution)/shard_map/ppermute | solution.py:314
  109.8 0.1 shard_map.86
  109.8 0.0 copy-start
  109.8 0.0 copy-start.1
  109.9 5.6 %collective-permute-start.7 = (bf16[128,1024]{1,0:T(8,128)(2,1)S(1)}, bf16[128,1024]{1,0:T(8,128)(2,1)S(1)}, u32[]{:S(2)}, u32[]{:S(2)}) collective-permute-start(bf16[128,1024]{1,0:T(8,128)(2,1)S(1)} %shard_map.86), channel_id=1, source_target_pairs={{0,14},{1,3},{2,0},{3,5},{4,2},{5,7},{6,4},{7,9},{8,6},{9,11},{10,... | collective-permute-start | bytes 786440 | tf_op jit(solution)/shard_map/ppermute | solution.py:314
  115.5 0.0 collective-permute-done.3.arrived_ref
  115.5 0.1 shard_map.84
  115.6 1.9 %collective-permute-start.4 = (bf16[128,1024]{1,0:T(8,128)(2,1)S(1)}, bf16[128,1024]{1,0:T(8,128)(2,1)S(1)}, u32[]{:S(2)}, u32[]{:S(2)}) collective-permute-start(bf16[128,1024]{1,0:T(8,128)(2,1)S(1)} %shard_map.84), channel_id=1, source_target_pairs={{0,2},{1,15},{2,4},{3,1},{4,6},{5,3},{6,8},{7,5},{8,10},{9,7},{10,... | collective-permute-start | bytes 786440 | tf_op jit(solution)/shard_map/ppermute | solution.py:312
  117.5 0.0 all-to-all-done.1
  117.5 1.3 shard_map.81
  118.8 2.5 %collective-permute-done.7 = bf16[128,1024]{1,0:T(8,128)(2,1)S(1)} collective-permute-done((bf16[128,1024]{1,0:T(8,128)(2,1)S(1)}, bf16[128,1024]{1,0:T(8,128)(2,1)S(1)}, u32[]{:S(2)}, u32[]{:S(2)}) %collective-permute-start.7) | collective-permute-done | bytes 262176 | tf_op jit(solution)/shard_map/ppermute | solution.py:314
  121.3 3.7 %collective-permute-done.4 = bf16[128,1024]{1,0:T(8,128)(2,1)S(1)} collective-permute-done((bf16[128,1024]{1,0:T(8,128)(2,1)S(1)}, bf16[128,1024]{1,0:T(8,128)(2,1)S(1)}, u32[]{:S(2)}, u32[]{:S(2)}) %collective-permute-start.4) | collective-permute-done | bytes 262176 | tf_op jit(solution)/shard_map/ppermute | solution.py:312
  125.0 0.8 fusion.2
  (3 shorter events, 0.0 us)
Async XLA Ops:
  67.5 4.8 %collective-permute-start = (bf16[3072,128]{1,0:T(8,128)(2,1)S(1)}, bf16[3072,128]{1,0:T(8,128)(2,1)S(1)}, u32[]{:S(2)}, u32[]{:S(2)}) collective-permute-start(bf16[3072,128]{1,0:T(8,128)(2,1)S(1)} %bitcast.15), channel_id=1, source_target_pairs={{0,1},{1,0},{2,3},{3,2},{4,5},{5,4},{6,7},{7,6},{8,9},{9,8},{10,11... | collective-permute-start | bytes 2359304 | tf_op jit(solution)/shard_map/ppermute | solution.py:242
  76.1 15.6 %collective-permute-start.1 = (bf16[128,1024]{1,0:T(8,128)(2,1)S(1)}, bf16[128,1024]{1,0:T(8,128)(2,1)S(1)}, u32[]{:S(2)}, u32[]{:S(2)}) collective-permute-start(bf16[128,1024]{1,0:T(8,128)(2,1)S(1)} %get-tuple-element.16), channel_id=1, source_target_pairs={{0,2},{1,15},{2,4},{3,1},{4,6},{5,3},{6,8},{7,5},{8,10},{9,7},{10,... | collective-permute-start | bytes 786440 | tf_op jit(solution)/shard_map/ppermute | solution.py:312
  80.5 37.0 %all-to-all-start.1 = ((bf16[64,24,128]{2,1,0:T(8,128)(2,1)}), bf16[64,24,128]{2,1,0:T(8,128)(2,1)S(1)}, u32[]{:S(2)}, u32[]{:S(2)}) async-start(bf16[64,24,128]{2,1,0:T(8,128)(2,1)} %bitcast.8), calls=%async_computation.1 | async-start | bytes 786432 | tf_op jit(solution)/shard_map/all_to_all | solution.py:319
  87.2 10.3 %collective-permute-start.5 = (bf16[128,1024]{1,0:T(8,128)(2,1)S(1)}, bf16[128,1024]{1,0:T(8,128)(2,1)S(1)}, u32[]{:S(2)}, u32[]{:S(2)}) collective-permute-start(bf16[128,1024]{1,0:T(8,128)(2,1)S(1)} %get-tuple-element.18), channel_id=1, source_target_pairs={{0,14},{1,3},{2,0},{3,5},{4,2},{5,7},{6,4},{7,9},{8,6},{9,11},{10,... | collective-permute-start | bytes 786440 | tf_op jit(solution)/shard_map/ppermute | solution.py:314
  91.7 11.4 %collective-permute-start.2 = (bf16[128,1024]{1,0:T(8,128)(2,1)S(1)}, bf16[128,1024]{1,0:T(8,128)(2,1)S(1)}, u32[]{:S(2)}, u32[]{:S(2)}) collective-permute-start(bf16[128,1024]{1,0:T(8,128)(2,1)S(1)} %shard_map.82), channel_id=1, source_target_pairs={{0,2},{1,15},{2,4},{3,1},{4,6},{5,3},{6,8},{7,5},{8,10},{9,7},{10,... | collective-permute-start | bytes 786440 | tf_op jit(solution)/shard_map/ppermute | solution.py:312
  97.5 12.3 %collective-permute-start.6 = (bf16[128,1024]{1,0:T(8,128)(2,1)S(1)}, bf16[128,1024]{1,0:T(8,128)(2,1)S(1)}, u32[]{:S(2)}, u32[]{:S(2)}) collective-permute-start(bf16[128,1024]{1,0:T(8,128)(2,1)S(1)} %shard_map.85), channel_id=1, source_target_pairs={{0,14},{1,3},{2,0},{3,5},{4,2},{5,7},{6,4},{7,9},{8,6},{9,11},{10,... | collective-permute-start | bytes 786440 | tf_op jit(solution)/shard_map/ppermute | solution.py:314
  103.2 12.3 %collective-permute-start.3 = (bf16[128,1024]{1,0:T(8,128)(2,1)S(1)}, bf16[128,1024]{1,0:T(8,128)(2,1)S(1)}, u32[]{:S(2)}, u32[]{:S(2)}) collective-permute-start(bf16[128,1024]{1,0:T(8,128)(2,1)S(1)} %shard_map.83), channel_id=1, source_target_pairs={{0,2},{1,15},{2,4},{3,1},{4,6},{5,3},{6,8},{7,5},{8,10},{9,7},{10,... | collective-permute-start | bytes 786440 | tf_op jit(solution)/shard_map/ppermute | solution.py:312
  109.8 7.7 %copy-start = (s32[128,1]{0,1:T(1,128)S(1)}, s32[128,1]{0,1:T(1,128)}, u32[]{:S(2)}) copy-start(s32[128,1]{0,1:T(1,128)} %param.8) | copy-start | bytes 1540
  109.8 7.7 %copy-start.1 = (f32[128,1]{0,1:T(1,128)S(1)}, f32[128,1]{0,1:T(1,128)}, u32[]{:S(2)}) copy-start(f32[128,1]{0,1:T(1,128)} %param.9) | copy-start | bytes 1540
  109.9 11.4 %collective-permute-start.7 = (bf16[128,1024]{1,0:T(8,128)(2,1)S(1)}, bf16[128,1024]{1,0:T(8,128)(2,1)S(1)}, u32[]{:S(2)}, u32[]{:S(2)}) collective-permute-start(bf16[128,1024]{1,0:T(8,128)(2,1)S(1)} %shard_map.86), channel_id=1, source_target_pairs={{0,14},{1,3},{2,0},{3,5},{4,2},{5,7},{6,4},{7,9},{8,6},{9,11},{10,... | collective-permute-start | bytes 786440 | tf_op jit(solution)/shard_map/ppermute | solution.py:314
  115.6 9.5 %collective-permute-start.4 = (bf16[128,1024]{1,0:T(8,128)(2,1)S(1)}, bf16[128,1024]{1,0:T(8,128)(2,1)S(1)}, u32[]{:S(2)}, u32[]{:S(2)}) collective-permute-start(bf16[128,1024]{1,0:T(8,128)(2,1)S(1)} %shard_map.84), channel_id=1, source_target_pairs={{0,2},{1,15},{2,4},{3,1},{4,6},{5,3},{6,8},{7,5},{8,10},{9,7},{10,... | collective-permute-start | bytes 786440 | tf_op jit(solution)/shard_map/ppermute | solution.py:312
